TPU v7x, 32 devices: a whole 2x2x4 slice. The times are simulated.
32 devices in a mesh: dp: 8 (over y, x, core), mp: 4 (over z).
Axes of the slice: x: 2, y: 2, z: 4, core: 2. Of those that a mesh axis runs over, the one named last changes fastest.
Arguments:
- image_rows: bfloat16 [100352, 384], P(('dp', 'mp')), may hold values from -5.375 to 5.375
- tall_weight: float32 [51, 5, 384], replicated, may hold values from -0.75 to 0.75
- wide_weight: float32 [5, 51, 384], replicated, may hold values from -0.75 to 0.75
- small_weight: float32 [5, 5, 384], replicated, may hold values from -0.75 to 0.75
- tall_mask: int32 [51, 5, 384], replicated, may hold values 0 or 1
- wide_mask: int32 [5, 51, 384], replicated, may hold values 0 or 1
- small_mask: int32 [5, 5, 384], replicated, may hold values 0 or 1
- bn_gain: float32 [384], replicated, may hold values from 0.3 to 3
- bn_bias: float32 [384], replicated, may hold values from -3 to 3
- ln_gain: float32 [384], replicated, may hold values from 0.5 to 1.5
- ln_bias: float32 [384], replicated, may hold values from -3 to 3
- fc1_weight: bfloat16 [384, 1536], P(None, 'mp'), may hold values from -0.3125 to 0.3125
- fc1_bias: float32 [1536], replicated, may hold values from -3 to 3
- fc2_weight: bfloat16 [1536, 384], P('mp'), may hold values from -0.21875 to 0.21875
- fc2_bias: float32 [384], replicated, may hold values from -3 to 3
- layer_scale: float32 [384], replicated, may hold values from 0.5 to 1.5
- out_grad: bfloat16 [100352, 384], P(('dp', 'mp')), may hold values from -4 to 4
Outputs:
- block_out: bfloat16 [100352, 384], P(('dp', 'mp'))
- in_grad: bfloat16 [100352, 384], P(('dp', 'mp'))
- tall_grad: float32 [51, 5, 384], replicated
- wide_grad: float32 [5, 51, 384], replicated
- small_grad: float32 [5, 5, 384], replicated
- bn_gain_grad: float32 [384], replicated
- bn_bias_grad: float32 [384], replicated
- ln_gain_grad: float32 [384], replicated
- ln_bias_grad: float32 [384], replicated
- fc1_grad: float32 [384, 1536], P(None, 'mp')
- fc1_bias_grad: float32 [1536], P('mp')
- fc2_grad: float32 [1536, 384], P('mp')
- fc2_bias_grad: float32 [384], replicated
- scale_grad: float32 [384], replicated
All inputs are finite; a program needn't handle non-finite values.
Results may differ from a plain program's by a relative error of at most 0.0079.
Values may be sent and summed in bfloat16 or wider, within the bound.
No kernel may reach another device: no remote copies, remote signals or barrier semaphores. Data moves between devices by JAX's collectives and lax.ppermute only.
A program may use at most 448 MiB of HBM per device.

v0:
```python
from functools import partial

import jax
import jax.numpy as jnp
import numpy as np
from jax import lax
from jax.sharding import PartitionSpec as P

MAP = 14
PIX = 196
LONGK = 51
SHORTK = 5
SMALLK = 5


norm_epsilon = 1e-05
layer_epsilon = 1e-06
highest = lax.Precision.HIGHEST


def tap_tables():
    coords = np.arange(MAP)
    row_of = np.repeat(coords, MAP)
    col_of = np.tile(coords, MAP)
    delta_rows = row_of[None, :] - row_of[:, None]
    delta_cols = col_of[None, :] - col_of[:, None]
    half_long = LONGK // 2
    half_short = SHORTK // 2
    half_small = SMALLK // 2
    sentinel = 2 * LONGK * SHORTK + SMALLK * SMALLK
    tall_valid = (np.abs(delta_rows) <= half_long) & (np.abs(delta_cols) <= half_short)
    tall_index = np.where(
        tall_valid, (delta_rows + half_long) * SHORTK + delta_cols + half_short, sentinel
    )
    wide_valid = (np.abs(delta_rows) <= half_short) & (np.abs(delta_cols) <= half_long)
    wide_index = np.where(
        wide_valid,
        LONGK * SHORTK + (delta_rows + half_short) * LONGK + delta_cols + half_long,
        sentinel,
    )
    small_valid = (np.abs(delta_rows) <= half_small) & (np.abs(delta_cols) <= half_small)
    small_index = np.where(
        small_valid,
        2 * LONGK * SHORTK + (delta_rows + half_small) * SMALLK + delta_cols + half_small,
        sentinel,
    )
    return (tall_index.astype(np.int32), wide_index.astype(np.int32), small_index.astype(np.int32))


def kernel_matrix(tall_live, wide_live, small_live):
    channels = tall_live.shape[-1]
    tap_table = jnp.concatenate(
        [
            tall_live.reshape(-1, channels),
            wide_live.reshape(-1, channels),
            small_live.reshape(-1, channels),
            jnp.zeros((1, channels), jnp.float32),
        ],
        axis=0,
    )
    tall_index, wide_index, small_index = tap_tables()
    return tap_table[tall_index] + tap_table[wide_index] + tap_table[small_index]


def offset_taps(d_kernel):
    channels = d_kernel.shape[-1]
    span = 2 * MAP - 1
    offsets = np.arange(span) - (MAP - 1)
    coords = np.arange(MAP)
    diagonal_pick = (
        coords[None, None, :] - coords[None, :, None] == offsets[:, None, None]
    ).astype(np.float32)
    grid_five = d_kernel.reshape(MAP, MAP, MAP, MAP, channels)
    by_rows = jnp.einsum("oik,ijklc->ojlc", diagonal_pick, grid_five, precision=highest)
    taps_grid = jnp.einsum("pjl,ojlc->opc", diagonal_pick, by_rows, precision=highest)
    centre = MAP - 1
    half_long = LONGK // 2
    half_short = SHORTK // 2
    half_small = SMALLK // 2
    margin = half_long - centre
    tall_part = jnp.pad(
        taps_grid[:, centre - half_short : centre + half_short + 1],
        ((margin, margin), (0, 0), (0, 0)),
    )
    wide_part = jnp.pad(
        taps_grid[centre - half_short : centre + half_short + 1, :],
        ((0, 0), (margin, margin), (0, 0)),
    )
    small_part = taps_grid[
        centre - half_small : centre + half_small + 1, centre - half_small : centre + half_small + 1
    ]
    return (tall_part, wide_part, small_part)


def conv_apply(kernel, images):
    result = lax.dot_general(
        kernel, images, (((1,), (1,)), ((2,), (2,))), preferred_element_type=jnp.float32
    )
    return jnp.transpose(result, (2, 1, 0))


def conv_back(kernel, grad_images):
    result = lax.dot_general(
        kernel, grad_images, (((0,), (1,)), ((2,), (2,))), preferred_element_type=jnp.float32
    )
    return jnp.transpose(result, (2, 1, 0))


def kernel_back(grad_images, images):
    result = lax.dot_general(
        grad_images, images, (((0,), (0,)), ((2,), (2,))), preferred_element_type=jnp.float32
    )
    return jnp.transpose(result, (1, 2, 0))


def on_device(
    image_rows,
    tall_weight,
    wide_weight,
    small_weight,
    tall_mask,
    wide_mask,
    small_mask,
    bn_gain,
    bn_bias,
    ln_gain,
    ln_bias,
    fc1_weight,
    fc1_bias,
    fc2_weight,
    fc2_bias,
    layer_scale,
    out_grad,
):
    row_count = image_rows.shape[0]
    channels = image_rows.shape[1]
    total_rows = row_count * lax.axis_size("dp") * lax.axis_size("mp")
    images = image_rows.reshape(-1, PIX, channels)
    tall_keep = tall_mask.astype(jnp.float32)
    wide_keep = wide_mask.astype(jnp.float32)
    small_keep = small_mask.astype(jnp.float32)
    built = kernel_matrix(
        tall_weight * tall_keep, wide_weight * wide_keep, small_weight * small_keep
    )
    kernel = built.astype(jnp.bfloat16)
    conv = conv_apply(kernel, images).reshape(row_count, channels)
    moments = lax.psum((jnp.sum(conv, axis=0), jnp.sum(conv * conv, axis=0)), ("dp", "mp"))
    mean_conv = moments[0] / total_rows
    variance = moments[1] / total_rows - mean_conv * mean_conv
    bn_inv = lax.rsqrt(variance + norm_epsilon)
    bn_hat = (conv - mean_conv) * bn_inv
    bn_out = bn_hat * bn_gain + bn_bias
    center = bn_out - jnp.mean(bn_out, axis=-1, keepdims=True)
    ln_inv = lax.rsqrt(jnp.mean(center * center, axis=-1, keepdims=True) + layer_epsilon)
    ln_hat = center * ln_inv
    normed = (ln_hat * ln_gain + ln_bias).astype(jnp.bfloat16)
    gelu_tanh = partial(jax.nn.gelu, approximate=True)
    shard_width = fc1_weight.shape[1]
    bias_shard = lax.dynamic_slice_in_dim(fc1_bias, lax.axis_index("mp") * shard_width, shard_width)
    group_rows = lax.all_gather(normed, "mp", axis=0, tiled=True)
    hidden = jnp.dot(group_rows, fc1_weight, preferred_element_type=jnp.float32) + bias_shard
    active_full, gelu_pull = jax.vjp(gelu_tanh, hidden)
    active = active_full.astype(jnp.bfloat16)
    row_piece = lax.slice_in_dim(active, 0, row_count * lax.axis_size("mp"), axis=0)
    project = lax.psum_scatter(
        jnp.dot(row_piece, fc2_weight, preferred_element_type=jnp.float32),
        "mp",
        scatter_dimension=0,
        tiled=True,
    )
    mixed = project + fc2_bias
    block_out = (image_rows.astype(jnp.float32) + layer_scale * mixed).astype(jnp.bfloat16)
    grad_rows = out_grad.astype(jnp.float32)
    scale_part = jnp.sum(grad_rows * mixed, axis=0)
    d_mixed = grad_rows * layer_scale
    bias_two_part = jnp.sum(d_mixed, axis=0)
    d_project = d_mixed.astype(jnp.bfloat16)
    group_grad = lax.all_gather(d_project, "mp", axis=0, tiled=True)
    d_active = lax.dot_general(
        group_grad, fc2_weight, (((1,), (1,)), ((), ())), preferred_element_type=jnp.float32
    )
    fc2_part = lax.dot_general(
        active, group_grad, (((0,), (0,)), ((), ())), preferred_element_type=jnp.float32
    )
    d_hidden = gelu_pull(d_active)[0].astype(jnp.bfloat16)
    fc1_part = lax.dot_general(
        group_rows, d_hidden, (((0,), (0,)), ((), ())), preferred_element_type=jnp.float32
    )
    bias_one_part = jnp.sum(d_hidden.astype(jnp.float32), axis=0)
    row_piece = d_hidden
    d_normed = lax.psum_scatter(
        lax.dot_general(
            row_piece, fc1_weight, (((1,), (1,)), ((), ())), preferred_element_type=jnp.float32
        ),
        "mp",
        scatter_dimension=0,
        tiled=True,
    )
    fc1_grad, fc2_grad, fc1_bias_grad = lax.psum((fc1_part, fc2_part, bias_one_part), "dp")
    ln_gain_part = jnp.sum(d_normed * ln_hat, axis=0)
    ln_bias_part = jnp.sum(d_normed, axis=0)
    d_hat = d_normed * ln_gain
    d_bn_out = ln_inv * (
        d_hat
        - jnp.mean(d_hat, axis=-1, keepdims=True)
        - ln_hat * jnp.mean(d_hat * ln_hat, axis=-1, keepdims=True)
    )
    bn_gain_grad, bn_bias_grad = lax.psum(
        (jnp.sum(d_bn_out * bn_hat, axis=0), jnp.sum(d_bn_out, axis=0)), ("dp", "mp")
    )
    d_conv = (
        bn_gain
        * bn_inv
        * (d_bn_out - bn_bias_grad / total_rows - bn_hat * bn_gain_grad / total_rows)
    ).astype(jnp.bfloat16)
    grad_images = d_conv.reshape(-1, PIX, channels)
    in_grad = (conv_back(kernel, grad_images).reshape(row_count, channels) + grad_rows).astype(
        jnp.bfloat16
    )
    d_kernel = kernel_back(grad_images, images)
    tall_part, wide_part, small_part = offset_taps(d_kernel)
    sums = lax.psum(
        (
            tall_part * tall_keep,
            wide_part * wide_keep,
            small_part * small_keep,
            ln_gain_part,
            ln_bias_part,
            scale_part,
            bias_two_part,
        ),
        ("dp", "mp"),
    )
    return (
        block_out,
        in_grad,
        sums[0],
        sums[1],
        sums[2],
        bn_gain_grad,
        bn_bias_grad,
        sums[3],
        sums[4],
        fc1_grad,
        fc1_bias_grad,
        fc2_grad,
        sums[6],
        sums[5],
    )


def solution(mesh):
    placed = (
        P(("dp", "mp"), None),
        P(),
        P(),
        P(),
        P(),
        P(),
        P(),
        P(),
        P(),
        P(),
        P(),
        P(None, "mp"),
        P(),
        P("mp", None),
        P(),
        P(),
        P(("dp", "mp"), None),
    )
    return jax.shard_map(
        on_device,
        mesh=mesh,
        in_specs=placed,
        out_specs=(
            P(("dp", "mp"), None),
            P(("dp", "mp"), None),
            P(),
            P(),
            P(),
            P(),
            P(),
            P(),
            P(),
            P(None, "mp"),
            P("mp"),
            P("mp", None),
            P(),
            P(),
        ),
        check_vma=False,
    )
```

profile of v0, /device:TPU:0, one launch (start us, length us, event | category | flops | bytes accessed | tf_op | source)
XLA Modules:
  0.0 1609.8 jit_solution(13851173964685515288)
XLA Ops:
  7.3 3.7 fusion.13
  12.6 94.8 %gather_fusion = f32[38416,384]{1,0:T(8,128)} fusion(f32[536,384]{1,0:T(8,128)S(1)} %maximum_maximum_fusion, s32[38912]{0:T(1024)S(1)} %pad_clamp_fusion.2), kind=kCustom, calls=%fused_computation | custom fusion | bytes 118167616 | tf_op jit(solution)/shard_map/gather | solution.py:62
  107.4 94.6 %gather_fusion.1 = f32[38416,384]{1,0:T(8,128)} fusion(f32[536,384]{1,0:T(8,128)S(1)} %maximum_maximum_fusion, s32[38912]{0:T(1024)S(1)} %copy-done.11), kind=kCustom, calls=%fused_computation.1 | custom fusion | bytes 118167616 | tf_op jit(solution)/shard_map/gather | solution.py:62
  202.0 94.7 %gather_fusion.2 = f32[38416,384]{1,0:T(8,128)} fusion(f32[536,384]{1,0:T(8,128)S(1)} %maximum_maximum_fusion, s32[38912]{0:T(1024)S(1)} %pad_clamp_fusion), kind=kCustom, calls=%fused_computation.2 | custom fusion | bytes 118167616 | tf_op jit(solution)/shard_map/gather | solution.py:62
  296.7 63.4 %add_convert_fusion = bf16[38416,384]{1,0:T(8,128)(2,1)} fusion(f32[38416,384]{1,0:T(8,128)} %gather_fusion.2, f32[38416,384]{1,0:T(8,128)} %gather_fusion, f32[38416,384]{1,0:T(8,128)} %gather_fusion.1), kind=kLoop, calls=%fused_computation.5 | loop fusion | flops 44255232 | bytes 206524416 | tf_op jit(solution)/shard_map/convert_element_type | solution.py:145
  360.2 37.1 %reshape.173 = bf16[196,196,384]{2,1,0:T(8,128)(2,1)} reshape(bf16[38416,384]{1,0:T(8,128)(2,1)} %add_convert_fusion) | data formatting | bytes 59006976 | tf_op jit(solution)/shard_map/convert_element_type | solution.py:145
  397.3 49.0 %copy.52 = bf16[196,196,384]{1,0,2:T(8,128)(2,1)} copy(bf16[196,196,384]{2,1,0:T(8,128)(2,1)} %reshape.173) | data formatting | bytes 59006976 | tf_op jit(solution)/shard_map/convert_element_type | solution.py:145
  446.3 2.1 reshape.139
  448.4 4.0 copy.53
  452.4 19.5 %multiply_reduce_fusion.1 = (f32[384]{0:T(512)S(1)}, f32[384,196,16]{1,2,0:T(8,128)}) fusion(bf16[196,196,384]{1,0,2:T(8,128)(2,1)} %copy.52, bf16[16,196,384]{1,0,2:T(8,128)(2,1)S(1)} %copy.53), kind=kOutput, calls=%fused_computation.27 | convolution fusion | flops 474463872 | bytes 36730368 | tf_op jit(solution)/shard_map/dot_general | solution.py:96
  471.9 3.8 reduce_sum.117
  475.8 42.3 %all-reduce.4 = (f32[384]{0:T(512)S(1)}, f32[384]{0:T(512)S(1)}) all-reduce(f32[384]{0:T(512)S(1)} %get-tuple-element.72, f32[384]{0:T(512)S(1)} %reduce_sum.117), channel_id=1, replica_groups=mesh['dp'=8,'mp'=4] {'dp','mp'}, use_global_device_ids=true, to_apply=%region_3.0 | all-reduce | flops 768 | bytes 6144 | tf_op jit(solution)/shard_map/psum | solution.py:147
  518.1 4.4 fusion.16
  522.6 4.4 multiply_reduce_fusion
  527.2 7.6 reshape.178
  534.8 5.9 copy.66
  540.7 4.5 add_convert_fusion.2
  546.0 13.7 fusion.25
  559.8 155.4 %all-gather.3.cloned.1.call-done = bf16[12544,384]{1,0:T(8,128)(2,1)} async-done(((bf16[3136,384]{1,0:T(8,128)(2,1)}), bf16[12544,384]{1,0:T(8,128)(2,1)}) %all-gather.3.cloned.1.call-update) | async-done | bytes 9633808 | tf_op jit(solution)/shard_map/all_gather | solution.py:160
  715.2 26.2 %convert_reduce_fusion = (f32[384]{0:T(512)}, bf16[12544,384]{1,0:T(8,128)(2,1)S(1)}, bf16[12544,384]{1,0:T(8,128)(2,1)}) fusion(f32[12544,384]{1,0:T(8,128)} %fusion.25, f32[384]{0:T(512)S(1)} %dynamic_slice.3, bf16[12544,384]{1,0:T(8,128)(2,1)} %all-gather.3.cloned.1.call-done, bf16[384,384]{1,0:T(8,128)(2,1)S(1)} %copy-done), kind=kOutput, calls=%fused_computation.16 | convolution fusion | flops 3819798016 | bytes 48466944 | tf_op jit(solution)/shard_map/dot_general | solution.py:161
  741.4 3.7 copy-done.1
  745.1 10.5 fusion.26
  755.7 12.2 fusion.24
  767.9 12.5 fusion.27
  780.5 293.6 %reduce-scatter.5.cloned.1.call-done = f32[3136,384]{1,0:T(8,128)} async-done(((f32[12544,384]{1,0:T(8,128)}), f32[3136,384]{1,0:T(8,128)}) %reduce-scatter.5.cloned.1.call-update) | async-done | bytes 4816912 | tf_op jit(solution)/shard_map/reduce_scatter | solution.py:191
  1074.0 7.5 multiply_reduce_fusion.2
  1081.6 7.5 fusion.22
  1089.1 45.8 %all-reduce.3 = (f32[384]{0:T(512)S(1)}, f32[384]{0:T(512)S(1)}) all-reduce(f32[384]{0:T(512)S(1)} %get-tuple-element.47, f32[384]{0:T(512)S(1)} %get-tuple-element.46), channel_id=1, replica_groups=mesh['dp'=8,'mp'=4] {'dp','mp'}, use_global_device_ids=true, to_apply=%region_13.0 | all-reduce | flops 768 | bytes 6144 | tf_op jit(solution)/shard_map/psum | solution.py:208
  1134.9 6.6 multiply_convert_fusion.1
  1141.5 4.1 reshape.141
  1145.5 5.1 copy.56
  1150.6 30.6 %convolution_bitcast_fusion = f32[196,196,384]{1,0,2:T(8,128)} fusion(bf16[16,196,384]{1,0,2:T(8,128)(2,1)} %copy.56, bf16[16,196,384]{1,0,2:T(8,128)(2,1)S(1)} %copy.53), kind=kOutput, calls=%fused_computation.6 | convolution fusion | flops 472055808 | bytes 63823872 | tf_op jit(solution)/shard_map/dot_general | solution.py:110
  1181.2 70.7 %copy.60 = f32[196,196,384]{2,1,0:T(8,128)} copy(f32[196,196,384]{1,0,2:T(8,128)} %convolution_bitcast_fusion) | data formatting | bytes 118013952 | tf_op jit(solution)/shard_map/transpose | solution.py:113
  1251.9 60.5 %reshape.143 = f32[14,14,14,14,384]{4,3,2,1,0:T(8,128)} reshape(f32[196,196,384]{2,1,0:T(8,128)} %copy.60) | data formatting | bytes 118013952 | tf_op jit(solution)/shard_map/reshape | solution.py:73
  1312.4 70.4 %fusion = f32[27,14,14,384,1]{3,0,4,2,1:T(8,128)S(1)} fusion(f32[27,14,14,1,1]{0,2,1,4,3:T(8,128)S(1)} %copy-done.21, f32[14,14,14,14,384]{4,3,2,1,0:T(8,128)} %reshape.143), kind=kOutput, calls=%fused_computation.3 | convolution fusion | flops 4779565056 | bytes 67156656 | tf_op jit(solution)/shard_map/oik,ijklc->ojlc/dot_general | solution.py:74
  1382.9 12.1 fusion.17
  1398.4 12.8 fusion.28
  1411.2 13.1 psum.108
  1425.8 17.3 %convolution_bitcast_fusion.1 = f32[16,196,384]{1,0,2:T(8,128)} fusion(bf16[196,196,384]{1,0,2:T(8,128)(2,1)} %copy.52, bf16[16,196,384]{1,0,2:T(8,128)(2,1)S(1)} %copy-done.2), kind=kOutput, calls=%fused_computation.43 | convolution fusion | flops 472055808 | bytes 36728832 | tf_op jit(solution)/shard_map/dot_general | solution.py:103
  1443.1 7.6 reshape.179
  1450.7 6.0 copy.67
  1456.8 6.9 fusion.15
  1463.7 42.0 %all-reduce.2 = (f32[5,5,384]{2,1,0:T(8,128)}, f32[384]{0:T(512)}, f32[384]{0:T(512)}, f32[384]{0:T(512)}, f32[384]{0:T(512)}) all-reduce(f32[5,5,384]{2,1,0:T(8,128)S(1)} %copy-done.16, f32[384]{0:T(512)S(1)} %copy-done.27, f32[384]{0:T(512)S(1)} %copy-done.28, ...), channel_id=1, replica_groups=mesh['dp'=8,'mp'=4] {'dp','mp'}, use_global_device_ids=true, to_apply=%region_16.0 | all-reduce | flops 11136 | bytes 89088 | tf_op jit(solution)/shard_map/psum | solution.py:222
  1505.7 29.8 %all-reduce.10.cloned.1.call-done = (f32[51,5,384]{2,1,0:T(8,128)}, f32[5,51,384]{2,1,0:T(8,128)}) async-done(((f32[51,5,384]{2,1,0:T(8,128)}, f32[5,51,384]{2,1,0:T(8,128)}), (f32[51,5,384]{2,1,0:T(8,128)}, f32[5,51,384]{2,1,0:T(8,128)})) %all-reduce.10.cloned.1.call-update) | async-done | bytes 783376 | tf_op jit(solution)/shard_map/psum | solution.py:222
  1535.6 1.9 copy.61
  1537.5 59.8 %all-reduce.12.cloned.1.call-done = (f32[384,384]{1,0:T(8,128)}, f32[384,384]{1,0:T(8,128)}) async-done(((f32[384,384]{1,0:T(8,128)}, f32[384,384]{1,0:T(8,128)}), (f32[384,384]{1,0:T(8,128)}, f32[384,384]{1,0:T(8,128)})) %all-reduce.12.cloned.1.call-update) | async-done | bytes 1179664 | tf_op jit(solution)/shard_map/psum | solution.py:199
  1599.0 1.9 copy.87
  1600.9 1.9 copy.88
  (106 shorter events, 9.4 us)
Async XLA Ops:
  7.2 708.0 %copy-start = (bf16[384,384]{1,0:T(8,128)(2,1)S(1)}, bf16[384,384]{1,0:T(8,128)(2,1)}, u32[]{:S(2)}) copy-start(bf16[384,384]{1,0:T(8,128)(2,1)} %param.36) | copy-start | bytes 884740
  7.2 4.4 copy-start.17
  7.2 4.5 copy-start.19
  7.2 3.9 copy-start.13
  7.2 3.9 copy-start.9
  7.2 4.2 copy-start.12
  7.3 4.2 copy-start.7
  7.3 4.3 copy-start.23
  7.3 4.3 copy-start.14
  7.3 538.8 %all-gather.5.cloned.1.call-start = ((), (), s32[]{:S(2)}) async-start(), calls=%async_computation.4 | async-start | bytes 12042240 | tf_op jit(solution)/shard_map/all_gather | solution.py:178
  11.1 704.1 %all-gather.3.cloned.1.call-start = ((), (), s32[]{:S(2)}) async-start(), calls=%async_computation.2 | async-start | bytes 12042240 | tf_op jit(solution)/shard_map/all_gather | solution.py:160
  12.6 94.8 %copy-start.11 = (s32[38912]{0:T(1024)S(1)}, s32[38912]{0:T(1024)}, u32[]{:S(2)}) copy-start(s32[38912]{0:T(1024)} %pad_clamp_fusion.1) | copy-start | bytes 466948
  107.4 94.6 %copy-start.18 = (s32[38416]{0:T(1024)S(1)}, s32[38416]{0:T(1024)}, u32[]{:S(2)}) copy-start(s32[38416]{0:T(1024)} %constant.69) | copy-start | bytes 460996
  397.3 49.0 %copy-start.5 = (bf16[3136,384]{1,0:T(8,128)(2,1)S(1)}, bf16[3136,384]{1,0:T(8,128)(2,1)}, u32[]{:S(2)}) copy-start(bf16[3136,384]{1,0:T(8,128)(2,1)} %param.25) | copy-start | bytes 7225348
  471.9 46.1 %copy-start.22 = (f32[384]{0:T(512)S(1)}, f32[384]{0:T(512)}, u32[]{:S(2)}) copy-start(f32[384]{0:T(512)} %param.32) | copy-start | bytes 4612
  471.9 46.1 %copy-start.24 = (f32[384]{0:T(512)S(1)}, f32[384]{0:T(512)}, u32[]{:S(2)}) copy-start(f32[384]{0:T(512)} %param.33) | copy-start | bytes 4612
  534.8 5.9 copy-start.25
  534.8 5.9 copy-start.32
  545.2 528.8 %reduce-scatter.5.cloned.1.call-start = ((), (), s32[]{:S(2)}) async-start(), calls=%async_computation.5 | async-start | bytes 24084480 | tf_op jit(solution)/shard_map/reduce_scatter | solution.py:191
  741.4 3.7 copy-start.1
  755.6 701.1 %reduce-scatter.3.cloned.1.call-start = ((), (), s32[]{:S(2)}) async-start(), calls=%async_computation.3 | async-start | bytes 24084480 | tf_op jit(solution)/shard_map/reduce_scatter | solution.py:165
  767.9 767.7 %all-reduce.10.cloned.1.call-start = ((), (), s32[]{:S(2)}) async-start(), calls=%async_computation.6 | async-start | bytes 2113536 | tf_op jit(solution)/shard_map/psum | solution.py:222
  1074.0 7.5 copy-start.3
  1134.9 10.6 copy-start.30
  1134.9 10.6 copy-start.33
  1251.9 60.5 %copy-start.21 = (f32[27,14,14,1,1]{0,2,1,4,3:T(8,128)S(1)}, f32[27,14,14,1,1]{0,2,1,4,3:T(8,128)}, u32[]{:S(2)}) copy-start(f32[27,14,14,1,1]{0,2,1,4,3:T(8,128)} %constant.70) | copy-start | bytes 63508
  1312.4 70.4 %copy-start.20 = (f32[27,14,14,1]{0,2,1,3:T(8,128)S(1)}, f32[27,14,14,1]{0,2,1,3:T(8,128)}, u32[]{:S(2)}) copy-start(f32[27,14,14,1]{0,2,1,3:T(8,128)} %constant.71) | copy-start | bytes 63508
  1382.9 13.2 copy-start.8
  1382.9 14.0 copy-start.10
  1395.0 1.1 copy-start.6
  1397.9 13.3 copy-start.31
  1397.9 26.5 %copy-start.15 = (s32[5,5,384]{2,1,0:T(8,128)S(1)}, s32[5,5,384]{2,1,0:T(8,128)}, u32[]{:S(2)}) copy-start(s32[5,5,384]{2,1,0:T(8,128)} %param.31) | copy-start | bytes 115204
  1397.9 27.9 %copy-start.2 = (bf16[16,196,384]{1,0,2:T(8,128)(2,1)S(1)}, bf16[16,196,384]{1,0,2:T(8,128)(2,1)}, u32[]{:S(2)}) copy-start(bf16[16,196,384]{1,0,2:T(8,128)(2,1)} %copy.56) | copy-start | bytes 7225348
  1397.9 199.3 %all-reduce.12.cloned.1.call-start = ((), (), s32[]{:S(2)}) async-start(), calls=%async_computation.7 | async-start | bytes 2359296 | tf_op jit(solution)/shard_map/psum | solution.py:199
  1450.7 6.1 copy-start.4
  1450.7 6.1 copy-start.26
  1450.7 6.1 copy-start.29
  1456.8 6.9 copy-start.16
  1456.8 6.9 copy-start.27
  1456.8 6.9 copy-start.28
Sparse Core Ops, SparseCore 0:
  11.2 172.6 all-gather.4
  545.3 169.7 all-gather.2
  755.8 318.2 reduce-scatter.4
  1076.3 322.1 reduce-scatter.2
  1404.5 131.0 all-reduce.9
  1539.5 57.6 all-reduce.11
where the time goes:
time: 1620 us; the launch traced here: 1610 us
  local copies, waits for them, and re-layouts  558 us (34%)
  waiting for transfers between devices  539 us (33%)
  matrix products  238 us (15%)
  blocking collectives  143 us (9%)
  other arithmetic  117 us (7%)
    reduce_scatter x1, waiting for transfers between devices, on_device(): lax.psum_scatter(lax.dot_general(row_piece, fc1_weight, (((1,), (1,)), ((...  294 us
    all_gather x1, waiting for transfers between devices, on_device(): group_rows = lax.all_gather(normed, 'mp', axis=0, tiled=True)  155 us
    gather x1, local copies, waits for them, and re-layouts, kernel_matrix(): tap_table[tall_index] + tap_table[wide_index] + tap_table[small_index]  94.8 us
    gather x1, local copies, waits for them, and re-layouts, kernel_matrix(): tap_table[small_index]  94.7 us
    gather x1, local copies, waits for them, and re-layouts, kernel_matrix(): tap_table[wide_index]  94.6 us
    convert_element_type x2, local copies, waits for them, and re-layouts, on_device(): kernel = built.astype(jnp.bfloat16)  86.1 us
    transpose x1, local copies, waits for them, and re-layouts, kernel_back(): return jnp.transpose(result, (1, 2, 0))  70.7 us
    dot_general x1, matrix products, offset_taps(): jnp.einsum('oik,ijklc->ojlc', diagonal_pick, grid_five, precision=highest)  70.4 us
  transfers between devices with their start and end apart: 6, of which 4 were waited for; matrix products, arithmetic and copies ran while one was open for 54% of the time, Pallas kernels for 0%

commit v1 on v0

v1 whole, which is shorter than its diff:
```python
import jax
import jax.numpy as jnp
import numpy as np
from jax import lax
from jax.experimental import pallas as pl
from jax.experimental.pallas import tpu as pltpu
from jax.sharding import PartitionSpec as P

MAP = 14
PIX = MAP * MAP
D = 384
LONG_LO = 25 - (MAP - 1)
SPAN = 2 * MAP - 1
BN_EPS = 1e-05
LN_EPS = 1e-06

NFREQ = 368
FROWS = 2 * NFREQ
GROUP = 4 * PIX
STEP = 2 * GROUP
WIN = 208
WIN_AT = tuple(16 * (PIX * m // 16) for m in range(4))
NTAPS = 256
REST = 245
SIDE = MAP - 3

TILE = 448
CHUNK = 256
GELU_ROWS = 64
NORM_ROWS = 112
LAST_ROWS = 112
SET = 13
FREQ_ROWS = 16
VMEM_LIMIT = 60 * 1024 * 1024
SMALL_VMEM = 4 * 1024 * 1024
FINISH_VMEM = 12 * 1024 * 1024


def tap_offsets():
    taps = [(a, b) for b in range(-2, 3) for a in range(1 - MAP, MAP)]
    for a in range(-2, 3):
        taps += [(a, b) for b in range(1 - MAP, MAP) if abs(b) > 2]
    return np.array(taps)


def bf16_pair(x):
    high = np.asarray(x, np.float32).astype(jnp.bfloat16)
    low = (np.asarray(x, np.float64) - high.astype(np.float64)).astype(np.float32).astype(jnp.bfloat16)
    return np.stack([high, low])


def transform_tables():
    freq = [
        (u, v)
        for u in range(SPAN)
        for v in range(SPAN)
        if (u, v) <= ((-u) % SPAN, (-v) % SPAN)
    ]
    freq = np.array(freq)
    count = len(freq)
    twice = np.where((freq == 0).all(axis=1), 1.0, 2.0)

    def angles(points):
        return 2 * np.pi * ((freq @ points.T) % SPAN) / SPAN

    pixels = np.stack([np.repeat(np.arange(MAP), MAP), np.tile(np.arange(MAP), MAP)], axis=1)
    theta = angles(pixels)
    forward = np.zeros((4, FROWS, WIN))
    for m in range(4):
        at = PIX * m - WIN_AT[m]
        forward[m, :count, at : at + PIX] = np.cos(theta)
        forward[m, NFREQ : NFREQ + count, at : at + PIX] = -np.sin(theta)
    inverse = np.zeros((PIX, FROWS))
    inverse[:, :count] = twice * np.cos(theta).T
    inverse[:, NFREQ : NFREQ + count] = -twice * np.sin(theta).T
    taps = tap_offsets()
    phi = angles(taps)
    from_taps = np.zeros((FROWS, NTAPS))
    from_taps[:count, : len(taps)] = np.cos(phi)
    from_taps[NFREQ : NFREQ + count, : len(taps)] = np.sin(phi)
    to_taps = np.zeros((NTAPS, FROWS))
    to_taps[: len(taps), :count] = twice * np.cos(phi).T
    to_taps[: len(taps), NFREQ : NFREQ + count] = twice * np.sin(phi).T
    as_bf16 = lambda x: x.astype(np.float32).astype(jnp.bfloat16)
    return as_bf16(forward), as_bf16(inverse), bf16_pair(from_taps), bf16_pair(to_taps)


def dot(a, b):
    return jnp.dot(a, b, preferred_element_type=jnp.float32)


def dot_t(a, b):
    return lax.dot_general(a, b, (((1,), (1,)), ((), ())), preferred_element_type=jnp.float32)


def as_float(x):
    return x.astype(jnp.float32)


def as_row(ref):
    return ref[...].reshape(1, -1)


def fold8(x):
    return jnp.sum(x.reshape(-1, 8, x.shape[-1]), axis=0)


def pair_window(ref, m):
    return jnp.concatenate(
        [ref[g * GROUP + WIN_AT[m] : g * GROUP + WIN_AT[m] + WIN, :] for g in range(2)],
        axis=1,
    )


def put_pair(ref, m, pair):
    for g in range(2):
        at = g * GROUP + PIX * m
        ref[at : at + PIX, :] = pair[:, g * D : (g + 1) * D]


def whole(a):
    return pl.BlockSpec(a.shape, lambda i, n=len(a.shape): (0,) * n)


def start_all(copies):
    for copy in copies:
        copy.start()


def wait_all(copies):
    for copy in copies:
        copy.wait()


def conv_kernel(
    image_ref, tall_ref, wide_ref, small_ref, tall_mask_ref, wide_mask_ref, small_mask_ref,
    forward_ref, inverse_ref, from_taps_ref,
    conv_ref, khat_ref, moments_ref,
    product_ref, taps_ref, sums_ref,
):
    step = pl.program_id(0)

    @pl.when(step == 0)
    def _():
        sums_ref[...] = jnp.zeros_like(sums_ref)
        taps_ref[...] = jnp.zeros_like(taps_ref)
        for b in range(5):
            column = tall_ref[b, LONG_LO : LONG_LO + SPAN] * as_float(tall_mask_ref[b, LONG_LO : LONG_LO + SPAN])
            middle = column[MAP - 3 : MAP + 2] + wide_ref[:, 23 + b, :] * as_float(wide_mask_ref[:, 23 + b, :])
            middle = middle + small_ref[:, b, :] * as_float(small_mask_ref[:, b, :])
            taps_ref[SPAN * b : SPAN * b + SPAN, :] = column
            taps_ref[SPAN * b + MAP - 3 : SPAN * b + MAP + 2, :] = middle
        for r in range(5):
            at = 5 * SPAN + 2 * SIDE * r
            for lo in (LONG_LO, 28):
                row = wide_ref[r, lo : lo + SIDE] * as_float(wide_mask_ref[r, lo : lo + SIDE])
                taps_ref[at : at + SIDE, :] = row
                at += SIDE
        taps = taps_ref[...].astype(jnp.bfloat16)
        khat = dot(from_taps_ref[0], taps) + dot(from_taps_ref[1], taps)
        khat_ref[...] = khat * np.float32(1.0 / (SPAN * SPAN))

    for k in range(2):
        images = (2 * k, 2 * k + 1)
        spectra = [dot(forward_ref[m], pair_window(image_ref, m)) for m in images]
        for r in range(0, NFREQ, FREQ_ROWS):
            re, im = slice(r, r + FREQ_ROWS), slice(NFREQ + r, NFREQ + r + FREQ_ROWS)
            real, imag = khat_ref[re, :], khat_ref[im, :]
            for m, xhat in zip(images, spectra):
                for g in range(2):
                    cols = slice(g * D, (g + 1) * D)
                    xr, xi = xhat[re, cols], xhat[im, cols]
                    product_ref[m, re, cols] = (real * xr - imag * xi).astype(jnp.bfloat16)
                    product_ref[m, im, cols] = (real * xi + imag * xr).astype(jnp.bfloat16)
        for m in images:
            put_pair(conv_ref, m, dot(inverse_ref[...], product_ref[m]))
    conv = conv_ref[...]
    sums_ref[:8, :] += fold8(conv)
    sums_ref[8:, :] += fold8(conv * conv)

    @pl.when(step == pl.num_programs(0) - 1)
    def _():
        sums = [jnp.sum(sums_ref[8 * i : 8 * i + 8, :], axis=0, keepdims=True) for i in range(2)]
        put_everywhere(moments_ref, jnp.concatenate(sums, axis=0))


def conv_forward(image_rows, weights, masks, tables):
    rows = image_rows.shape[0]
    steps = rows // STEP
    forward, inverse, from_taps, _ = tables
    khat = jax.ShapeDtypeStruct((FROWS, D), jnp.float32)
    devices = lax.axis_size("dp") * lax.axis_size("mp")
    moments = jax.ShapeDtypeStruct((devices, 2, D), jnp.float32)
    return pl.pallas_call(
        conv_kernel,
        grid=(steps,),
        in_specs=[pl.BlockSpec((STEP, D), lambda i: (i, 0))]
        + [whole(a) for a in (*weights, *masks, forward, inverse, from_taps)],
        out_specs=[
            pl.BlockSpec((STEP, D), lambda i: (i, 0)),
            whole(khat),
            whole(moments),
        ],
        out_shape=[
            jax.ShapeDtypeStruct((rows, D), jnp.float32),
            khat,
            moments,
        ],
        scratch_shapes=[
            pltpu.VMEM((4, FROWS, 2 * D), jnp.bfloat16),
            pltpu.VMEM((NTAPS, D), jnp.float32),
            pltpu.VMEM((16, D), jnp.float32),
        ],
        compiler_params=pltpu.CompilerParams(vmem_limit_bytes=VMEM_LIMIT),
        cost_estimate=pl.CostEstimate(
            flops=4 * rows * D * FROWS, bytes_accessed=rows * D * 10, transcendentals=0
        ),
        name="conv_forward",
    )(image_rows, *weights, *masks, forward, inverse, from_taps)


def put_everywhere(ref, rows):
    ref[...] = jnp.broadcast_to(rows[None], ref.shape)


def arrived(ref):
    return jnp.sum(ref[...], axis=0)


def exchange(x):
    return lax.all_to_all(x, ("dp", "mp"), split_axis=0, concat_axis=0)


def batch_norm_terms(moments_ref, total):
    moments = arrived(moments_ref)
    mean = moments[0:1, :] * np.float32(1.0 / total)
    variance = moments[1:2, :] * np.float32(1.0 / total) - mean * mean
    return mean, lax.rsqrt(variance + BN_EPS)


def split_refs(refs):
    return (*refs[:3], refs[3 : 3 + SET], refs[3 + SET : 3 + 2 * SET], *refs[3 + 2 * SET :])


def mlp_kernel(total, *refs):
    blocks = lax.axis_size("mp")
    conv_hbm, image_hbm, grad_hbm, moments_ref = refs[:4]
    vectors, refs = [as_row(ref) for ref in refs[4:11]], refs[11:]
    own, direct, other = refs[:2], refs[2 : 1 + blocks], refs[1 + blocks : 2 * blocks]
    out_hbm, dbn_hbm, gw_hbm, bn_sums_ref, vec_ref = refs[2 * blocks : 5 + 2 * blocks]
    (
        conv_all, image_all, grad_all, set_a, set_b, w1_ref, w2_ref, mixed_ref, dnormed_ref, g1_ref, g2_ref,
        gw_ref, sum_ref, tile_sems, weight_sems, gw_sems,
    ) = split_refs(refs[5 + 2 * blocks :])
    rows = conv_all.shape[0]
    tiles = rows // TILE
    hidden = blocks * D
    core, place = lax.axis_index("dp") % 2, lax.axis_index("mp")

    def rows_of_tile(t):
        return pl.ds(pl.multiple_of(t * TILE, TILE), TILE)

    def reads(t):
        at = rows_of_tile(t)
        pairs = [(conv_hbm, conv_all), (grad_hbm, grad_all), (image_hbm, image_all)]
        return [
            pltpu.make_async_copy(a.at[at], b.at[at], tile_sems.at[i, t]) for i, (a, b) in enumerate(pairs)
        ]

    def writes(t, buffers):
        at = rows_of_tile(t)
        pairs = [(buffers[3], out_hbm), (buffers[4], dbn_hbm)]
        return [
            pltpu.make_async_copy(a, b.at[at], tile_sems.at[3 + i, t]) for i, (a, b) in enumerate(pairs)
        ]

    start_all(reads(0))

    def weight_copies(first, second):
        copies = []
        for s in range(blocks):
            at = slice(s * D, (s + 1) * D)
            source = (own[0], own[1]) if s == 0 else (first[s - 1], second[s - 1])
            copies.append(pltpu.make_async_copy(source[0], w1_ref.at[:, at], weight_sems.at[0, s]))
            copies.append(pltpu.make_async_copy(source[1], w2_ref.at[at, :], weight_sems.at[1, s]))
        return copies

    @pl.when(core == 0)
    def _():
        start_all(weight_copies(direct, other))

    @pl.when(core != 0)
    def _():
        start_all(weight_copies(other, direct))

    for t in range(1, tiles):
        start_all(reads(t))

    mean, bn_inv = batch_norm_terms(moments_ref, total)
    bn_gain, bn_bias, ln_gain, ln_bias, fc2_bias, layer_scale, fc1_bias = vectors
    scale = bn_inv * bn_gain
    bias_of = [fc1_bias[:, i * D : (i + 1) * D] for i in range(blocks)]
    bias = jnp.concatenate(
        [sum(jnp.where((place ^ s) == i, bias_of[i], 0.0) for i in range(blocks)) for s in range(blocks)], axis=1
    )
    sum_ref[...] = jnp.zeros_like(sum_ref)
    g1_ref[...] = jnp.zeros_like(g1_ref)
    g2_ref[...] = jnp.zeros_like(g2_ref)
    ones_row = jnp.where(lax.broadcasted_iota(jnp.int32, (16, TILE), 0) == 0, 1.0, 0.0).astype(jnp.bfloat16)
    set_a[7][D:, :] = ones_row
    set_b[7][D:, :] = ones_row

    def wide(x):
        return jnp.broadcast_to(x, (x.shape[0], 128))

    def across(x):
        return jnp.concatenate([x] * (D // 128), axis=1)

    def fetch(t, buffers):
        wait_all(reads(t))
        at = rows_of_tile(t)
        for whole, buffer in zip((conv_all, grad_all, image_all), buffers):
            buffer[...] = whole[at, :]

    def normalize(buffers):
        conv_ref, grad_ref = buffers[:2]
        normed_ref, dproj_ref, normed_t_ref, dproj_t_ref, mu_ref, inv_ref = buffers[5:11]
        for r in range(0, TILE, NORM_ROWS):
            at = slice(r, r + NORM_ROWS)
            out = (conv_ref[at, :] - mean) * scale + bn_bias
            mu = jnp.mean(out, axis=1, keepdims=True)
            center = out - mu
            inv = lax.rsqrt(jnp.mean(center * center, axis=1, keepdims=True) + LN_EPS)
            mu_ref[at, :] = wide(mu)
            inv_ref[at, :] = wide(inv)
            normed_ref[at, :] = (center * inv * ln_gain + ln_bias).astype(jnp.bfloat16)
            grad = as_float(grad_ref[at, :])
            dproj_ref[at, :] = (grad * layer_scale).astype(jnp.bfloat16)
            sum_ref[40:48, :] += fold8(grad)
        normed_t_ref[:D, :] = jnp.transpose(normed_ref[...])
        dproj_t_ref[...] = jnp.transpose(dproj_ref[...])

    root = np.float32(np.sqrt(2.0 / np.pi))
    cubic = np.float32(0.044715 * np.sqrt(2.0 / np.pi))

    def gelu_chunk(c, buffers):
        normed_ref, dproj_ref, act_ref, dhid_ref = buffers[5], buffers[6], buffers[11], buffers[12]
        cols = slice(c * CHUNK, (c + 1) * CHUNK)
        hid_all = dot(normed_ref[...], w1_ref[:, cols])
        dact_all = dot_t(dproj_ref[...], w2_ref[cols, :])
        for r in range(0, TILE, GELU_ROWS):
            hid = hid_all[r : r + GELU_ROWS] + bias[:, cols]
            square = hid * hid
            th = jnp.tanh(hid * (root + cubic * square))
            half = 0.5 + 0.5 * th
            act = hid * half
            slope = half + act * (1.0 - th) * (root + 3 * cubic * square)
            act_ref[r : r + GELU_ROWS, cols] = act.astype(jnp.bfloat16)
            dhid_ref[r : r + GELU_ROWS, cols] = (dact_all[r : r + GELU_ROWS] * slope).astype(jnp.bfloat16)

    def finish_rows(r, buffers):
        conv_ref, grad_ref, image_ref, out_ref, dbn_ref = buffers[:5]
        mu_ref, inv_ref = buffers[9:11]
        at = slice(r, r + LAST_ROWS)
        mixed = mixed_ref[at, :] + fc2_bias
        dnormed = dnormed_ref[at, :]
        out_ref[at, :] = (as_float(image_ref[at, :]) + layer_scale * mixed).astype(jnp.bfloat16)
        conv = conv_ref[at, :] - mean
        bn_hat = conv * bn_inv
        inv = across(inv_ref[at, :])
        ln_hat = (conv * scale + bn_bias - across(mu_ref[at, :])) * inv
        d_hat = dnormed * ln_gain
        first = jnp.mean(d_hat, axis=1, keepdims=True)
        second = jnp.mean(d_hat * ln_hat, axis=1, keepdims=True)
        dbn = inv * (d_hat - first - ln_hat * second)
        dbn_ref[at, :] = dbn
        sum_ref[0:8, :] += fold8(dbn * bn_hat)
        sum_ref[8:16, :] += fold8(dbn)
        sum_ref[16:24, :] += fold8(dnormed * ln_hat)
        sum_ref[24:32, :] += fold8(dnormed)
        sum_ref[32:40, :] += fold8(as_float(grad_ref[at, :]) * mixed)

    chunks = hidden // CHUNK
    parts = TILE // LAST_ROWS

    def step(ahead, now):
        if now is not None:
            act_ref, dhid_ref = now[11:13]
            mixed_ref[...] = dot(act_ref[...], w2_ref[...])
            dnormed_ref[...] = dot_t(dhid_ref[...], w1_ref[...])
        if ahead is not None:
            normalize(ahead)
        for c in range(chunks):
            if ahead is not None:
                gelu_chunk(c, ahead)
            if now is not None:
                cols = slice(c * CHUNK, (c + 1) * CHUNK)
                g1_ref[:, cols] += dot(now[7][...], dhid_ref[:, cols])
                g2_ref[:, cols] += dot(now[8][...], act_ref[:, cols])
                for i in range(c * parts // chunks, (c + 1) * parts // chunks):
                    finish_rows(i * LAST_ROWS, now)

    def two_steps(i, _):
        fetch(2 * i + 1, set_b)

        @pl.when(i > 0)
        def _():
            wait_all(writes(2 * i - 2, set_a))

        step(set_b, set_a)
        start_all(writes(2 * i, set_a))
        fetch(2 * i + 2, set_a)

        @pl.when(i > 0)
        def _():
            wait_all(writes(2 * i - 1, set_b))

        step(set_a, set_b)
        start_all(writes(2 * i + 1, set_b))
        return 0

    fetch(0, set_a)
    wait_all(weight_copies(direct, other))
    step(set_a, None)
    lax.fori_loop(0, (tiles - 1) // 2, two_steps, 0)
    last = tiles - 1
    if tiles % 2 == 0:
        fetch(last, set_b)
        if tiles > 2:
            wait_all(writes(last - 3, set_a))
        step(set_b, set_a)
        start_all(writes(last - 1, set_a))
        if tiles > 2:
            wait_all(writes(last - 2, set_b))
        step(None, set_b)
        start_all(writes(last, set_b))
    else:
        if tiles > 1:
            wait_all(writes(last - 2, set_a))
        step(None, set_a)
        start_all(writes(last, set_a))

    chips, size = gw_ref.shape[1] // 2, gw_ref.shape[2]
    gw_copy = lambda s: pltpu.make_async_copy(gw_ref.at[s], gw_hbm.at[:, s], gw_sems.at[s])
    for s in range(blocks):
        cols = slice(s * D, (s + 1) * D)
        vec_ref[pl.ds(4 + (place ^ s), 1), :] = g1_ref[D : D + 1, cols]
        for i in range(chips):
            rows_of = slice(i * size, (i + 1) * size)
            gw_ref[s, 2 * i] = g1_ref[rows_of, cols].astype(jnp.bfloat16)
            gw_ref[s, 2 * i + 1] = g2_ref[rows_of, cols].astype(jnp.bfloat16)
        gw_copy(s).start()

    sums = [jnp.sum(sum_ref[8 * i : 8 * i + 8, :], axis=0, keepdims=True) for i in range(6)]
    put_everywhere(bn_sums_ref, jnp.concatenate(sums[:2], axis=0))
    vec_ref[0:4, :] = jnp.concatenate(sums[2:5] + [sums[5] * layer_scale], axis=0)
    for s in range(blocks):
        gw_copy(s).wait()
    first_set, second_set = (set_a, set_b) if tiles % 2 == 1 else (set_b, set_a)
    if tiles > 1:
        wait_all(writes(last - 1, second_set))
    wait_all(writes(last, first_set))


def mlp(total, conv, image_rows, out_grad, moments, vectors, own, direct, other):
    rows = conv.shape[0]
    tiles = rows // TILE
    blocks, chips = lax.axis_size("mp"), lax.axis_size("dp") // 2
    hidden = blocks * D
    vmem, hbm = pl.BlockSpec(memory_space=pltpu.VMEM), pl.BlockSpec(memory_space=pl.ANY)
    f32, bf16 = jnp.float32, jnp.bfloat16
    return pl.pallas_call(
        lambda *refs: mlp_kernel(total, *refs),
        in_specs=[hbm] * 3 + [vmem] * 8 + [hbm] * (2 * blocks),
        out_specs=[hbm] * 3 + [vmem] * 2,
        out_shape=[
            jax.ShapeDtypeStruct((rows, D), bf16),
            jax.ShapeDtypeStruct((rows, D), f32),
            jax.ShapeDtypeStruct((2 * chips, blocks, D // chips, D), bf16),
            jax.ShapeDtypeStruct((2 * chips * blocks, 2, D), f32),
            jax.ShapeDtypeStruct((4 + blocks, D), f32),
        ],
        scratch_shapes=[
            pltpu.VMEM((rows, D), f32),
            pltpu.VMEM((rows, D), bf16),
            pltpu.VMEM((rows, D), bf16),
        ]
        + [
            pltpu.VMEM((TILE, D), f32),
            pltpu.VMEM((TILE, D), bf16),
            pltpu.VMEM((TILE, D), bf16),
            pltpu.VMEM((TILE, D), bf16),
            pltpu.VMEM((TILE, D), f32),
            pltpu.VMEM((TILE, D), bf16),
            pltpu.VMEM((TILE, D), bf16),
            pltpu.VMEM((D + 16, TILE), bf16),
            pltpu.VMEM((D, TILE), bf16),
            pltpu.VMEM((TILE, 128), f32),
            pltpu.VMEM((TILE, 128), f32),
            pltpu.VMEM((TILE, hidden), bf16),
            pltpu.VMEM((TILE, hidden), bf16),
        ]
        * 2
        + [pltpu.VMEM((D, hidden), bf16), pltpu.VMEM((hidden, D), bf16)]
        + [pltpu.VMEM((TILE, D), f32)] * 2
        + [
            pltpu.VMEM((D + 16, hidden), f32),
            pltpu.VMEM((D, hidden), f32),
            pltpu.VMEM((blocks, 2 * chips, D // chips, D), bf16),
            pltpu.VMEM((48, D), f32),
            pltpu.SemaphoreType.DMA((5, tiles)),
            pltpu.SemaphoreType.DMA((2, blocks)),
            pltpu.SemaphoreType.DMA((blocks,)),
        ],
        compiler_params=pltpu.CompilerParams(vmem_limit_bytes=VMEM_LIMIT),
        cost_estimate=pl.CostEstimate(
            flops=12 * rows * D * hidden, bytes_accessed=rows * D * 20, transcendentals=rows * hidden
        ),
        name="mlp",
    )(conv, image_rows, out_grad, moments, *vectors, *own, *direct, *other)


def conv_back_kernel(
    total, dbn_ref, conv_ref, grad_ref, image_ref, khat_ref, moments_ref, bn_sums_ref, vec_ref, bn_gain_ref,
    forward_ref, inverse_ref, to_taps_ref,
    in_grad_ref, taps_ref,
    dconv_ref, image_grad_ref, product_ref, dhat_ref, all_taps_ref,
):
    step = pl.program_id(0)
    mean, bn_inv = batch_norm_terms(moments_ref, total)
    bn_sums = arrived(bn_sums_ref) * np.float32(1.0 / total)
    gain = as_row(bn_gain_ref) * bn_inv
    slope, shift = bn_sums[0:1, :], bn_sums[1:2, :]

    @pl.when(step == 0)
    def _():
        dhat_ref[...] = jnp.zeros_like(dhat_ref)

    for r in range(0, STEP, LAST_ROWS):
        at = slice(r, r + LAST_ROWS)
        bn_hat = (conv_ref[at, :] - mean) * bn_inv
        dconv = gain * (dbn_ref[at, :] - shift - bn_hat * slope)
        dconv_ref[at, :] = dconv.astype(jnp.bfloat16)
    for k in range(2):
        images = (2 * k, 2 * k + 1)
        spectra = [dot(forward_ref[m], pair_window(dconv_ref, m)) for m in images]
        image_spectra = [dot(forward_ref[m], pair_window(image_ref, m)) for m in images]
        for r in range(0, NFREQ, FREQ_ROWS):
            re, im = slice(r, r + FREQ_ROWS), slice(NFREQ + r, NFREQ + r + FREQ_ROWS)
            real, imag = khat_ref[re, :], khat_ref[im, :]
            tap_re, tap_im = [], []
            for m, ghat, xhat in zip(images, spectra, image_spectra):
                for g in range(2):
                    cols = slice(g * D, (g + 1) * D)
                    gr, gi = ghat[re, cols], ghat[im, cols]
                    product_ref[m, re, cols] = (real * gr + imag * gi).astype(jnp.bfloat16)
                    product_ref[m, im, cols] = (real * gi - imag * gr).astype(jnp.bfloat16)
                    xr, xi = xhat[re, cols], xhat[im, cols]
                    tap_re.append(xr * gr + xi * gi)
                    tap_im.append(xr * gi - xi * gr)
            dhat_ref[re, :] += tree_sum(tap_re)
            dhat_ref[im, :] += tree_sum(tap_im)
        for m in images:
            put_pair(image_grad_ref, m, dot(inverse_ref[...], product_ref[m]))
    in_grad_ref[...] = (image_grad_ref[...] + as_float(grad_ref[...])).astype(jnp.bfloat16)

    @pl.when(step == pl.num_programs(0) - 1)
    def _():
        dhat = dhat_ref[...]
        high = dhat.astype(jnp.bfloat16)
        low = (dhat - as_float(high)).astype(jnp.bfloat16)
        taps = dot(to_taps_ref[0], high) + dot(to_taps_ref[0], low) + dot(to_taps_ref[1], high)
        all_taps_ref[...] = taps * np.float32(1.0 / (SPAN * SPAN))
        all_taps_ref[REST : REST + vec_ref.shape[0], :] = vec_ref[...]
        devices, size, _ = taps_ref.shape
        for i in range(devices):
            if i * size < NTAPS:
                taps_ref[i] = all_taps_ref[i * size : (i + 1) * size, :].astype(jnp.bfloat16)
            else:
                taps_ref[i] = jnp.zeros((size, D), jnp.bfloat16)


def conv_backward(total, dbn, conv, out_grad, image_rows, khat, moments, bn_sums, vec, bn_gain, tables):
    rows = conv.shape[0]
    steps = rows // STEP
    forward, inverse, _, to_taps = tables
    devices = lax.axis_size("dp") * lax.axis_size("mp")
    f32, bf16 = jnp.float32, jnp.bfloat16
    block = pl.BlockSpec((STEP, D), lambda i: (i, 0))
    taps = jax.ShapeDtypeStruct((devices, max(8, NTAPS // devices), D), bf16)
    return pl.pallas_call(
        lambda *refs: conv_back_kernel(total, *refs),
        grid=(steps,),
        in_specs=[block] * 4
        + [whole(a) for a in (khat, moments, bn_sums, vec, bn_gain, forward, inverse, to_taps)],
        out_specs=[block, whole(taps)],
        out_shape=[jax.ShapeDtypeStruct((rows, D), bf16), taps],
        scratch_shapes=[
            pltpu.VMEM((STEP, D), bf16),
            pltpu.VMEM((STEP, D), f32),
            pltpu.VMEM((4, FROWS, 2 * D), bf16),
            pltpu.VMEM((FROWS, D), f32),
            pltpu.VMEM((NTAPS, D), f32),
        ],
        compiler_params=pltpu.CompilerParams(vmem_limit_bytes=VMEM_LIMIT),
        cost_estimate=pl.CostEstimate(
            flops=4 * rows * D * FROWS, bytes_accessed=rows * D * 18, transcendentals=0
        ),
        name="conv_backward",
    )(dbn, conv, out_grad, image_rows, khat, moments, bn_sums, vec, bn_gain, forward, inverse, to_taps)


def finish_kernel(chips, *refs):
    mine, other = refs[:chips], refs[chips : 2 * chips]
    tall_mask_ref, wide_mask_ref, small_mask_ref, bn_sums_ref = refs[2 * chips : 2 * chips + 4]
    tall_ref, wide_ref, small_ref, fc1_ref, fc2_ref = refs[2 * chips + 4 : 2 * chips + 9]
    vector_refs, taps_ref, fc2_t_ref = refs[2 * chips + 9 : -2], refs[-2], refs[-1]
    core, chip = lax.axis_index("dp") % 2, lax.axis_index("dp") // 2
    places, place = lax.axis_size("mp"), lax.axis_index("mp")
    size, count = taps_ref.shape[0] // (2 * chips * places), D // chips
    for k in range(chips):
        at = pl.ds(pl.multiple_of((chip ^ k) * count, 8), count)
        mine_rows, other_rows = as_float(mine[k][...]), as_float(other[k][...])
        for s in range(places):
            for owner, rows in ((core, mine_rows), (1 - core, other_rows)):
                device = (2 * (chip ^ k) + owner) * places + (place ^ s)
                taps_ref[pl.ds(pl.multiple_of(device * size, 8), size), :] = rows[s * size : (s + 1) * size]

        @pl.when(core == 0)
        def _():
            fc1_ref[at, :] = mine_rows[places * size :]
            fc2_t_ref[at, :] = other_rows[places * size :]

        @pl.when(core != 0)
        def _():
            fc1_ref[at, :] = other_rows[places * size :]
            fc2_t_ref[at, :] = mine_rows[places * size :]

    fc2_ref[...] = jnp.transpose(fc2_t_ref[...])
    bn_sums = arrived(bn_sums_ref)
    rows = [bn_sums[0:1], bn_sums[1:2]] + [taps_ref[REST + i : REST + i + 1, :] for i in range(4)]
    rows.append(taps_ref[pl.ds(REST + 4 + place, 1), :])
    for ref, row in zip(vector_refs, rows):
        ref[...] = row.reshape(ref.shape)
    tall_ref[...] = jnp.zeros_like(tall_ref)
    wide_ref[...] = jnp.zeros_like(wide_ref)
    for b in range(5):
        column = taps_ref[SPAN * b : SPAN * b + SPAN, :]
        middle = column[MAP - 3 : MAP + 2, :]
        tall_ref[b, LONG_LO : LONG_LO + SPAN] = column * as_float(tall_mask_ref[b, LONG_LO : LONG_LO + SPAN])
        small_ref[:, b, :] = middle * as_float(small_mask_ref[:, b, :])
        wide_ref[:, 23 + b, :] = middle * as_float(wide_mask_ref[:, 23 + b, :])
    for r in range(5):
        at = 5 * SPAN + 2 * SIDE * r
        for lo in (LONG_LO, 28):
            wide_ref[r, lo : lo + SIDE] = taps_ref[at : at + SIDE, :] * as_float(wide_mask_ref[r, lo : lo + SIDE])
            at += SIDE


def finish(mine, other, masks, bn_sums):
    chips, places = len(mine), lax.axis_size("mp")
    size = (mine[0].shape[0] - D // chips) // places
    vmem = pl.BlockSpec(memory_space=pltpu.VMEM)
    square = jax.ShapeDtypeStruct((D, D), jnp.float32)
    return pl.pallas_call(
        lambda *refs: finish_kernel(chips, *refs),
        in_specs=[vmem] * (2 * chips + 4),
        out_specs=[vmem] * 12,
        out_shape=[jax.ShapeDtypeStruct(m.shape, jnp.float32) for m in masks] + [square, square]
        + [jax.ShapeDtypeStruct((D,), jnp.float32)] * 7,
        scratch_shapes=[pltpu.VMEM((2 * chips * places * size, D), jnp.float32), pltpu.VMEM((D, D), jnp.float32)],
        compiler_params=pltpu.CompilerParams(vmem_limit_bytes=FINISH_VMEM),
        name="finish",
    )(*mine, *other, *masks, bn_sums)


def swap(x, axis, bit):
    size = lax.axis_size(axis)
    return lax.ppermute(x, axis, [(i, i ^ bit) for i in range(size)])


def swap_places(parts):
    got = [swap(x, "mp", s + 1) for s, x in reversed(list(enumerate(parts)))]
    return got[::-1]


def tree_sum(terms):
    while len(terms) > 1:
        terms = [a + b for a, b in zip(terms[::2], terms[1::2])]
    return terms[0]


def plane_steps():
    return range(2, lax.axis_size("dp"), 2)


def first_weights(fc1_weight, fc2_weight):
    mine = jnp.where(lax.axis_index("dp") % 2 == 0, fc1_weight, fc2_weight)
    powers = [1 << i for i in range(lax.axis_size("mp").bit_length() - 1)]
    return {s: swap(mine, "mp", s) for s in reversed(powers)}


def other_weights(got):
    for s in range(1, lax.axis_size("mp")):
        if s not in got:
            high = 1 << (s.bit_length() - 1)
            got[s] = swap(got[high], "mp", s ^ high)
    return [got[s] for s in range(1, lax.axis_size("mp"))]


def reduce_weight_grads(parts):
    return lax.optimization_barrier(lax.psum_scatter(parts, "dp", scatter_dimension=0, tiled=False))


def message_kernel(taps_ref, weights_ref, own_ref, *message_refs):
    taps = jnp.sum(as_float(taps_ref[...]), axis=0)
    own_ref[...] = jnp.concatenate([taps, as_float(weights_ref[0])], axis=0)
    for s, ref in enumerate(message_refs):
        ref[...] = jnp.concatenate([taps, as_float(weights_ref[s + 1])], axis=0).astype(jnp.bfloat16)


def total_kernel(own_ref, *refs):
    got, total_ref = refs[:-1], refs[-1]
    size = (total_ref.shape[0] - own_ref.shape[0]) // len(got)
    rows = [own_ref[...]] + [as_float(ref[...]) for ref in got]
    weights = tree_sum([x[size:] for x in rows])
    total_ref[...] = jnp.concatenate([x[:size] for x in rows] + [weights], axis=0).astype(jnp.bfloat16)


def reduce_rest(taps, weights):
    places, size, count = lax.axis_size("mp"), taps.shape[1], weights.shape[1]
    vmem = pl.BlockSpec(memory_space=pltpu.VMEM)
    rows = lambda n, kind: jax.ShapeDtypeStruct((n, D), kind)
    own, *messages = pl.pallas_call(
        message_kernel,
        in_specs=[vmem] * 2,
        out_specs=[vmem] * places,
        out_shape=[rows(size + count, jnp.float32)] + [rows(size + count, jnp.bfloat16)] * (places - 1),
        compiler_params=pltpu.CompilerParams(vmem_limit_bytes=SMALL_VMEM),
        name="messages",
    )(exchange(taps), weights)
    got = swap_places(messages)
    mine = pl.pallas_call(
        total_kernel,
        in_specs=[vmem] * places,
        out_specs=vmem,
        out_shape=rows(places * size + count, jnp.bfloat16),
        compiler_params=pltpu.CompilerParams(vmem_limit_bytes=SMALL_VMEM),
        name="totals",
    )(own, *got)
    mine = [mine] + [swap(mine, "dp", s) for s in plane_steps()]
    return mine, [swap(x, "dp", 1) for x in mine]


def on_device(
    image_rows, tall_weight, wide_weight, small_weight, tall_mask, wide_mask, small_mask,
    bn_gain, bn_bias, ln_gain, ln_bias, fc1_weight, fc1_bias, fc2_weight, fc2_bias, layer_scale, out_grad,
):
    rows = image_rows.shape[0]
    total = rows * lax.axis_size("dp") * lax.axis_size("mp")
    tables = tuple(jnp.asarray(t) for t in transform_tables())
    turn = lambda x: jnp.swapaxes(x, 0, 1)
    masks = (turn(tall_mask), wide_mask, small_mask)
    first = first_weights(fc1_weight, fc2_weight)

    conv, khat, moments = conv_forward(
        image_rows, (turn(tall_weight), wide_weight, small_weight), masks, tables
    )
    khat, first = lax.optimization_barrier((khat, first))
    early = {s: swap(x, "dp", 1) for s, x in first.items()}
    moments, direct, early = lax.optimization_barrier((exchange(moments), other_weights(first), early))
    other = [early[s + 1] if s + 1 in early else swap(x, "dp", 1) for s, x in enumerate(direct)]
    block_out, dbn, gw, bn_sums, vec = mlp(
        total, conv, image_rows, out_grad, moments,
        (bn_gain, bn_bias, ln_gain, ln_bias, fc2_bias, layer_scale, fc1_bias),
        (fc1_weight, fc2_weight), direct, other,
    )
    bn_sums = exchange(bn_sums)
    weights = reduce_weight_grads(gw)
    in_grad, taps = conv_backward(total, dbn, conv, out_grad, image_rows, khat, moments, bn_sums, vec, bn_gain, tables)
    mine, other = reduce_rest(taps, weights)
    tall_grad, wide_grad, small_grad, fc1_grad, fc2_grad, *vec = finish(mine, other, masks, bn_sums)
    tall_grad = turn(tall_grad)
    return (
        block_out, in_grad, tall_grad, wide_grad, small_grad, vec[0], vec[1], vec[2], vec[3],
        fc1_grad, vec[6], fc2_grad, vec[5], vec[4],
    )


def solution(mesh):
    rows, none = P(("dp", "mp"), None), P()
    return jax.shard_map(
        on_device,
        mesh=mesh,
        in_specs=(rows,) + (none,) * 10 + (P(None, "mp"), none, P("mp", None), none, none, rows),
        out_specs=(rows, rows) + (none,) * 7 + (P(None, "mp"), P("mp"), P("mp", None), none, none),
        check_vma=False,
    )
```

time: 1620 us -> 158 us (0.10)
  local copies, waits for them, and re-layouts: 558 us -> 2.53 us
  waiting for transfers between devices: 539 us -> 22.2 us
  matrix products: 238 us -> 0 us
  blocking collectives: 143 us -> 23.3 us
  other arithmetic: 117 us -> 1.01 us
  Pallas kernels: 0 us -> 75.9 us
  starting transfers between devices: 0.71 us -> 18.4 us
    reduce_scatter x2 -> x1, waiting for transfers between devices: 294 us -> 8.25 us  [reduce_weight_grads(): lax.psum_scatter(parts, 'dp', scatter_dimension=0, tiled=False)]
    gather x3 -> x0, local copies, waits for them, and re-layouts: 284 us -> none  [the longest x1 94.8 us: kernel_matrix(): tap_table[tall_index] + tap_table[wide_index] + tap_table[small_index]]
    dot_general x11 -> x0, matrix products: 238 us -> none  [the longest x1 70.4 us: offset_taps(): jnp.einsum('oik,ijklc->ojlc', diagonal_pick, grid_five, precision=highest)]
    all_gather x2 -> x0, waiting for transfers between devices: 155 us -> none  [the longest x1 155 us: on_device(): group_rows = lax.all_gather(normed, 'mp', axis=0, tiled=True)]
    psum x4 -> x0, blocking collectives: 143 us -> none  [the longest x1 45.8 us: on_device(): lax.psum((jnp.sum(d_bn_out * bn_hat, axis=0), jnp.sum(d_bn_out, axis=0)),...]
    reshape x12 -> x0, local copies, waits for them, and re-layouts: 103 us -> none  [the longest x1 60.5 us: offset_taps(): grid_five = d_kernel.reshape(MAP, MAP, MAP, MAP, channels)]
    psum x2 -> x0, waiting for transfers between devices: 89.6 us -> none  [the longest x1 59.8 us: on_device(): lax.psum((fc1_part, fc2_part, bias_one_part), 'dp')]
    convert_element_type x2 -> x0, local copies, waits for them, and re-layouts: 86.1 us -> none  [on_device(): kernel = built.astype(jnp.bfloat16)]
  transfers between devices with their start and end apart: 6 -> 18, of which waited for: 4 -> 12; matrix products, arithmetic and copies ran while one was open for 54% -> 0% of each run, Pallas kernels for 0% -> 20%
where the time goes in v1:
time: 158 us; the launch traced here: 157 us
  Pallas kernels  75.9 us (48%)
  blocking collectives  23.3 us (15%)
  waiting for transfers between devices  22.2 us (14%)
  starting transfers between devices  18.4 us (12%)
  between operations  14.2 us (9%)
  local copies, waits for them, and re-layouts  2.53 us (2%)
    pallas_call x1, Pallas kernels, mlp(): pl.pallas_call(lambda *refs: mlp_kernel(total, *refs), in_specs=[hbm] * 3...  42.5 us
    all_to_all x2, blocking collectives, exchange(): return lax.all_to_all(x, ('dp', 'mp'), split_axis=0, concat_axis=0)  23.3 us
    pallas_call x1, Pallas kernels, conv_backward(): pl.pallas_call(lambda *refs: conv_back_kernel(total, *refs), grid=(steps,...  20.1 us
    ppermute x16, starting transfers between devices, swap(): return lax.ppermute(x, axis, [(i, i ^ bit) for i in range(size)])  15.8 us
    ppermute x16, waiting for transfers between devices, swap(): return lax.ppermute(x, axis, [(i, i ^ bit) for i in range(size)])  12.8 us
    pallas_call x1, Pallas kernels, conv_forward(): pl.pallas_call(conv_kernel, grid=(steps,), in_specs=[pl.BlockSpec((STEP,...  11.6 us
    reduce_scatter x1, waiting for transfers between devices, reduce_weight_grads(): lax.psum_scatter(parts, 'dp', scatter_dimension=0, tiled=False)  8.25 us
  transfers between devices with their start and end apart: 18, of which 12 were waited for; matrix products, arithmetic and copies ran while one was open for 0% of the time, Pallas kernels for 20%

profile of v1, /device:TPU:0, one launch (start us, length us, event | category | flops | bytes accessed | tf_op | source)
XLA Modules:
  0.0 157.5 jit_solution(3873383357510982817)
XLA Ops:
  7.2 0.0 reduce-scatter.2.cloned.1.call-start
  7.2 1.0 broadcast_select_fusion
  8.2 4.1 %collective-permute-start.1 = (bf16[384,384]{1,0:T(8,128)(2,1)S(1)}, bf16[384,384]{1,0:T(8,128)(2,1)S(1)}, u32[]{:S(2)}, u32[]{:S(2)}) collective-permute-start(bf16[384,384]{1,0:T(8,128)(2,1)S(1)} %broadcast_select_fusion), channel_id=1, source_target_pairs={{0,2},{1,3},{2,0},{3,1},{4,6},{5,7},{6,4},{7,5},{8,10},{9,11},{10,... | collective-permute-start | bytes 884744 | tf_op jit(solution)/shard_map/ppermute | solution.py:679
  12.3 1.6 %collective-permute-start = (bf16[384,384]{1,0:T(8,128)(2,1)S(1)}, bf16[384,384]{1,0:T(8,128)(2,1)S(1)}, u32[]{:S(2)}, u32[]{:S(2)}) collective-permute-start(bf16[384,384]{1,0:T(8,128)(2,1)S(1)} %broadcast_select_fusion), channel_id=1, source_target_pairs={{0,1},{1,0},{2,3},{3,2},{4,5},{5,4},{6,7},{7,6},{8,9},{9,8},{10,11... | collective-permute-start | bytes 884744 | tf_op jit(solution)/shard_map/ppermute | solution.py:679
  13.9 11.6 %conv_forward.1 = (f32[3136,384]{1,0:T(8,128)}, f32[736,384]{1,0:T(8,128)}, f32[32,2,384]{2,1,0:T(2,128)}) custom-call(bf16[3136,384]{1,0:T(8,128)(2,1)} %refs_3_.1, f32[5,51,384]{2,1,0:T(8,128)} %bitcast.7, f32[5,51,384]{2,1,0:T(8,128)} %wide_ref.1, f32[5,5,384]{2,1,0:T(8,128)} %small_ref.1, s32[5,51,384]{2,1,0:T(8,128)} %bitcast.4, s32[5,51,384]{2,1,0:T(8,128)} %refs_9_.4, ...), custom_call_target="tpu_custom_call" | custom-call | flops 3545235456 | bytes 12042240 | tf_op jit(solution)/shard_map/conv_forward/pallas_call | solution.py:194
  25.5 0.3 collective-permute-done.1.refs_14_
  25.8 0.2 collective-permute-done.refs_13_
  26.0 0.0 collective-permute-start.3
  26.0 0.5 collective-permute-start.4
  26.5 1.5 collective-permute-start.2
  28.0 12.7 %all_to_all.15.refs_3_.refs_5_ = f32[32,2,384]{2,1,0:T(2,128)} all-to-all(f32[32,2,384]{2,1,0:T(2,128)} %get-tuple-element.50), channel_id=1, replica_groups=mesh['dp'=8,'mp'=4] {'dp','mp'}, dimensions={0} | all-to-all | bytes 196608 | tf_op jit(solution)/shard_map/all_to_all | solution.py:231
  40.7 0.0 collective-permute-done.3.refs_16_
  40.7 0.0 copy-start.9
  40.7 0.0 collective-permute-done.2.refs_15_
  40.7 0.0 copy-start.10
  40.7 0.1 collective-permute-start.5
  40.8 1.6 collective-permute-done.5.refs_18_
  42.4 0.7 copy-done.11
  43.1 42.5 %mlp.1 = (bf16[3136,384]{1,0:T(8,128)(2,1)}, f32[3136,384]{1,0:T(8,128)}, bf16[8,4,96,384]{3,2,1,0:T(8,128)(2,1)}, f32[32,2,384]{2,1,0:T(2,128)}, f32[8,384]{1,0:T(8,128)}) custom-call(f32[3136,384]{1,0:T(8,128)} %get-tuple-element.49.refs_0_.refs_1_, bf16[3136,384]{1,0:T(8,128)(2,1)} %refs_3_.1, bf16[3136,384]{1,0:T(8,128)(2,1)} %refs_2_.3, ...), custom_call_target="tpu_custom_call" | custom-call | flops 22196256768 | bytes 24084480 | tf_op jit(solution)/shard_map/mlp/pallas_call | solution.py:472
  85.6 0.0 reduce-scatter.2.cloned.1.call-update
  85.6 0.9 copy-done.5
  86.4 10.6 %all_to_all.16.refs_6_.refs_11_ = f32[32,2,384]{2,1,0:T(2,128)} all-to-all(f32[32,2,384]{2,1,0:T(2,128)S(1)} %copy-done.5), channel_id=1, replica_groups=mesh['dp'=8,'mp'=4] {'dp','mp'}, dimensions={0} | all-to-all | bytes 196608 | tf_op jit(solution)/shard_map/all_to_all | solution.py:231
  97.1 20.1 %conv_backward.1 = (bf16[3136,384]{1,0:T(8,128)(2,1)}, bf16[32,8,384]{2,1,0:T(8,128)(2,1)}) custom-call(f32[3136,384]{1,0:T(8,128)} %get-tuple-element.61.refs_0_, f32[3136,384]{1,0:T(8,128)} %get-tuple-element.49.refs_0_.refs_1_, bf16[3136,384]{1,0:T(8,128)(2,1)} %refs_2_.3, bf16[3136,384]{1,0:T(8,128)(2,1)} %refs_3_.1, ...), custom_call_target="tpu_custom_call" | custom-call | flops 3545235456 | bytes 21676032 | tf_op jit(solution)/shard_map/conv_backward/pallas_call | solution.py:591
  117.2 2.6 %all-to-all-start.2 = ((bf16[32,8,384]{2,1,0:T(8,128)(2,1)}), bf16[32,8,384]{2,1,0:T(8,128)(2,1)S(1)}, u32[]{:S(2)}, u32[]{:S(2)}) async-start(bf16[32,8,384]{2,1,0:T(8,128)(2,1)} %get-tuple-element.66), calls=%async_computation.2 | async-start | bytes 393216 | tf_op jit(solution)/shard_map/all_to_all | solution.py:231
  119.8 8.2 %reduce-scatter.2.cloned.1.call-done = bf16[1,4,96,384]{3,2,1,0:T(8,128)(2,1)} async-done(((bf16[8,4,96,384]{3,2,1,0:T(8,128)(2,1)}), bf16[1,4,96,384]{3,2,1,0:T(8,128)(2,1)}) %reduce-scatter.2.cloned.1.call-update) | async-done | bytes 294928 | tf_op jit(solution)/shard_map/reduce_scatter | solution.py:712
  128.1 1.1 all-to-all-done.2.taps_ref
  129.1 1.0 copy-done.3
  130.1 0.1 messages.1
  130.2 0.9 collective-permute-start.6
  131.0 2.5 %collective-permute-start.7 = (bf16[104,384]{1,0:T(8,128)(2,1)S(1)}, bf16[104,384]{1,0:T(8,128)(2,1)S(1)}, u32[]{:S(2)}, u32[]{:S(2)}) collective-permute-start(bf16[104,384]{1,0:T(8,128)(2,1)S(1)} %get-tuple-element.70), channel_id=1, source_target_pairs={{0,2},{1,3},{2,0},{3,1},{4,6},{5,7},{6,4},{7,5},{8,10},{9,11},{10,... | collective-permute-start | bytes 239624 | tf_op jit(solution)/shard_map/ppermute | solution.py:679
  133.5 1.1 collective-permute-start.8
  134.6 0.9 collective-permute-done.6.refs_0_
  135.5 4.6 %collective-permute-done.7.refs_1_ = bf16[104,384]{1,0:T(8,128)(2,1)S(1)} collective-permute-done((bf16[104,384]{1,0:T(8,128)(2,1)S(1)}, bf16[104,384]{1,0:T(8,128)(2,1)S(1)}, u32[]{:S(2)}, u32[]{:S(2)}) %collective-permute-start.7) | collective-permute-done | bytes 79904 | tf_op jit(solution)/shard_map/ppermute | solution.py:679
  140.1 0.0 collective-permute-done.8.refs_2_
  140.2 1.5 collective-permute-start.11
  141.7 1.4 collective-permute-start.10
  143.1 0.6 collective-permute-start.9
  143.7 2.1 %collective-permute-done.11.refs_3_ = bf16[128,384]{1,0:T(8,128)(2,1)S(1)} collective-permute-done((bf16[128,384]{1,0:T(8,128)(2,1)S(1)}, bf16[128,384]{1,0:T(8,128)(2,1)S(1)}, u32[]{:S(2)}, u32[]{:S(2)}) %collective-permute-start.11) | collective-permute-done | bytes 98336 | tf_op jit(solution)/shard_map/ppermute | solution.py:679
  145.8 0.0 collective-permute-start.15
  145.8 1.0 collective-permute-done.10.refs_2_
  146.8 0.0 collective-permute-start.14
  146.8 0.9 collective-permute-done.9.refs_1_
  147.7 0.0 collective-permute-start.13
  147.7 0.0 collective-permute-done.12.refs_4_
  147.7 0.0 collective-permute-done.15.refs_7_
  147.7 0.4 collective-permute-done.14.refs_6_
  148.1 0.9 collective-permute-done.13.refs_5_
  149.0 1.6 %finish.1 = (f32[5,51,384]{2,1,0:T(8,128)}, f32[5,51,384]{2,1,0:T(8,128)}, f32[5,5,384]{2,1,0:T(8,128)}, f32[384,384]{1,0:T(8,128)}, f32[384,384]{1,0:T(8,128)},...) custom-call(bf16[128,384]{1,0:T(8,128)(2,1)S(1)} %totals.1.refs_0_, ...), custom_call_target="tpu_custom_call" | custom-call | tf_op jit(solution)/shard_map/finish/pallas_call | solution.py:665
  (22 shorter events, 0.1 us)
Async XLA Ops:
  7.2 120.9 %reduce-scatter.2.cloned.1.call-start = ((), (), s32[]{:S(2)}) async-start(), calls=%async_computation.4 | async-start | bytes 2654208 | tf_op jit(solution)/shard_map/reduce_scatter | solution.py:712
  8.2 17.5 %collective-permute-start.1 = (bf16[384,384]{1,0:T(8,128)(2,1)S(1)}, bf16[384,384]{1,0:T(8,128)(2,1)S(1)}, u32[]{:S(2)}, u32[]{:S(2)}) collective-permute-start(bf16[384,384]{1,0:T(8,128)(2,1)S(1)} %broadcast_select_fusion), channel_id=1, source_target_pairs={{0,2},{1,3},{2,0},{3,1},{4,6},{5,7},{6,4},{7,5},{8,10},{9,11},{10,... | collective-permute-start | bytes 884744 | tf_op jit(solution)/shard_map/ppermute | solution.py:679
  12.3 13.6 %collective-permute-start = (bf16[384,384]{1,0:T(8,128)(2,1)S(1)}, bf16[384,384]{1,0:T(8,128)(2,1)S(1)}, u32[]{:S(2)}, u32[]{:S(2)}) collective-permute-start(bf16[384,384]{1,0:T(8,128)(2,1)S(1)} %broadcast_select_fusion), channel_id=1, source_target_pairs={{0,1},{1,0},{2,3},{3,2},{4,5},{5,4},{6,7},{7,6},{8,9},{9,8},{10,11... | collective-permute-start | bytes 884744 | tf_op jit(solution)/shard_map/ppermute | solution.py:679
  25.8 16.6 %copy-start.6 = (bf16[384,384]{1,0:T(8,128)(2,1)}, bf16[384,384]{1,0:T(8,128)(2,1)S(1)}, u32[]{:S(2)}) copy-start(bf16[384,384]{1,0:T(8,128)(2,1)S(1)} %collective-permute-done.1.refs_14_) | copy-start | bytes 884740
  26.0 16.4 %copy-start.7 = (bf16[384,384]{1,0:T(8,128)(2,1)}, bf16[384,384]{1,0:T(8,128)(2,1)S(1)}, u32[]{:S(2)}) copy-start(bf16[384,384]{1,0:T(8,128)(2,1)S(1)} %collective-permute-done.refs_13_) | copy-start | bytes 884740
  26.0 14.7 %collective-permute-start.3 = (bf16[384,384]{1,0:T(8,128)(2,1)S(1)}, bf16[384,384]{1,0:T(8,128)(2,1)S(1)}, u32[]{:S(2)}, u32[]{:S(2)}) collective-permute-start(bf16[384,384]{1,0:T(8,128)(2,1)S(1)} %collective-permute-done.refs_13_), channel_id=1, source_target_pairs={{0,4},{4,0},{8,12},{12,8},{16,20},{20,16},{24,28},{28,24},{1,5},{5... | collective-permute-start | bytes 884744 | tf_op jit(solution)/shard_map/ppermute | solution.py:679
  26.0 14.7 %collective-permute-start.4 = (bf16[384,384]{1,0:T(8,128)(2,1)S(1)}, bf16[384,384]{1,0:T(8,128)(2,1)S(1)}, u32[]{:S(2)}, u32[]{:S(2)}) collective-permute-start(bf16[384,384]{1,0:T(8,128)(2,1)S(1)} %collective-permute-done.1.refs_14_), channel_id=1, source_target_pairs={{0,4},{4,0},{8,12},{12,8},{16,20},{20,16},{24,28},{28,24},{1,5},{5... | collective-permute-start | bytes 884744 | tf_op jit(solution)/shard_map/ppermute | solution.py:679
  26.5 14.2 %collective-permute-start.2 = (bf16[384,384]{1,0:T(8,128)(2,1)S(1)}, bf16[384,384]{1,0:T(8,128)(2,1)S(1)}, u32[]{:S(2)}, u32[]{:S(2)}) collective-permute-start(bf16[384,384]{1,0:T(8,128)(2,1)S(1)} %collective-permute-done.1.refs_14_), channel_id=1, source_target_pairs={{0,1},{1,0},{2,3},{3,2},{4,5},{5,4},{6,7},{7,6},{8,9},{9,8},{10,11... | collective-permute-start | bytes 884744 | tf_op jit(solution)/shard_map/ppermute | solution.py:679
  40.7 1.7 %copy-start.8 = (bf16[384,384]{1,0:T(8,128)(2,1)}, bf16[384,384]{1,0:T(8,128)(2,1)S(1)}, u32[]{:S(2)}) copy-start(bf16[384,384]{1,0:T(8,128)(2,1)S(1)} %collective-permute-done.3.refs_16_) | copy-start | bytes 884740
  40.7 1.7 %copy-start.9 = (bf16[384,384]{1,0:T(8,128)(2,1)}, bf16[384,384]{1,0:T(8,128)(2,1)S(1)}, u32[]{:S(2)}) copy-start(bf16[384,384]{1,0:T(8,128)(2,1)S(1)} %collective-permute-done.4.refs_17_) | copy-start | bytes 884740
  40.7 1.7 %copy-start.10 = (bf16[384,384]{1,0:T(8,128)(2,1)}, bf16[384,384]{1,0:T(8,128)(2,1)S(1)}, u32[]{:S(2)}) copy-start(bf16[384,384]{1,0:T(8,128)(2,1)S(1)} %collective-permute-done.2.refs_15_) | copy-start | bytes 884740
  40.7 1.6 %collective-permute-start.5 = (bf16[384,384]{1,0:T(8,128)(2,1)S(1)}, bf16[384,384]{1,0:T(8,128)(2,1)S(1)}, u32[]{:S(2)}, u32[]{:S(2)}) collective-permute-start(bf16[384,384]{1,0:T(8,128)(2,1)S(1)} %collective-permute-done.2.refs_15_), channel_id=1, source_target_pairs={{0,4},{4,0},{8,12},{12,8},{16,20},{20,16},{24,28},{28,24},{1,5},{5... | collective-permute-start | bytes 884744 | tf_op jit(solution)/shard_map/ppermute | solution.py:679
  42.4 0.7 copy-start.11
  85.5 0.9 copy-start.5
  97.1 51.9 %copy-start = (f32[32,2,384]{2,1,0:T(2,128)S(1)}, f32[32,2,384]{2,1,0:T(2,128)}, u32[]{:S(2)}) copy-start(f32[32,2,384]{2,1,0:T(2,128)} %all_to_all.16.refs_6_.refs_11_) | copy-start | bytes 294916
  97.1 51.9 %copy-start.1 = (s32[51,5,384]{2,0,1:T(8,128)S(1)}, s32[51,5,384]{2,0,1:T(8,128)}, u32[]{:S(2)}) copy-start(s32[51,5,384]{2,0,1:T(8,128)} %param.25) | copy-start | bytes 1175044
  97.1 51.9 %copy-start.2 = (s32[5,51,384]{2,1,0:T(8,128)S(1)}, s32[5,51,384]{2,1,0:T(8,128)}, u32[]{:S(2)}) copy-start(s32[5,51,384]{2,1,0:T(8,128)} %refs_9_.4) | copy-start | bytes 1175044
  97.1 51.9 %copy-start.4 = (s32[5,5,384]{2,1,0:T(8,128)S(1)}, s32[5,5,384]{2,1,0:T(8,128)}, u32[]{:S(2)}) copy-start(s32[5,5,384]{2,1,0:T(8,128)} %refs_10_.4) | copy-start | bytes 115204
  117.2 11.9 %all-to-all-start.2 = ((bf16[32,8,384]{2,1,0:T(8,128)(2,1)}), bf16[32,8,384]{2,1,0:T(8,128)(2,1)S(1)}, u32[]{:S(2)}, u32[]{:S(2)}) async-start(bf16[32,8,384]{2,1,0:T(8,128)(2,1)} %get-tuple-element.66), calls=%async_computation.2 | async-start | bytes 393216 | tf_op jit(solution)/shard_map/all_to_all | solution.py:231
  129.1 1.0 copy-start.3
  130.2 5.3 %collective-permute-start.6 = (bf16[104,384]{1,0:T(8,128)(2,1)S(1)}, bf16[104,384]{1,0:T(8,128)(2,1)S(1)}, u32[]{:S(2)}, u32[]{:S(2)}) collective-permute-start(bf16[104,384]{1,0:T(8,128)(2,1)S(1)} %get-tuple-element.69), channel_id=1, source_target_pairs={{0,1},{1,0},{2,3},{3,2},{4,5},{5,4},{6,7},{7,6},{8,9},{9,8},{10,11... | collective-permute-start | bytes 239624 | tf_op jit(solution)/shard_map/ppermute | solution.py:679
  131.0 9.1 %collective-permute-start.7 = (bf16[104,384]{1,0:T(8,128)(2,1)S(1)}, bf16[104,384]{1,0:T(8,128)(2,1)S(1)}, u32[]{:S(2)}, u32[]{:S(2)}) collective-permute-start(bf16[104,384]{1,0:T(8,128)(2,1)S(1)} %get-tuple-element.70), channel_id=1, source_target_pairs={{0,2},{1,3},{2,0},{3,1},{4,6},{5,7},{6,4},{7,5},{8,10},{9,11},{10,... | collective-permute-start | bytes 239624 | tf_op jit(solution)/shard_map/ppermute | solution.py:679
  133.5 6.6 %collective-permute-start.8 = (bf16[104,384]{1,0:T(8,128)(2,1)S(1)}, bf16[104,384]{1,0:T(8,128)(2,1)S(1)}, u32[]{:S(2)}, u32[]{:S(2)}) collective-permute-start(bf16[104,384]{1,0:T(8,128)(2,1)S(1)} %get-tuple-element.71), channel_id=1, source_target_pairs={{0,3},{1,2},{2,1},{3,0},{4,7},{5,6},{6,5},{7,4},{8,11},{9,10},{10,... | collective-permute-start | bytes 239624 | tf_op jit(solution)/shard_map/ppermute | solution.py:679
  140.2 5.6 %collective-permute-start.11 = (bf16[128,384]{1,0:T(8,128)(2,1)S(1)}, bf16[128,384]{1,0:T(8,128)(2,1)S(1)}, u32[]{:S(2)}, u32[]{:S(2)}) collective-permute-start(bf16[128,384]{1,0:T(8,128)(2,1)S(1)} %totals.1.refs_0_), channel_id=1, source_target_pairs={{0,24},{4,28},{8,16},{12,20},{16,8},{20,12},{24,0},{28,4},{1,25},{... | collective-permute-start | bytes 294920 | tf_op jit(solution)/shard_map/ppermute | solution.py:679
  141.7 5.2 %collective-permute-start.10 = (bf16[128,384]{1,0:T(8,128)(2,1)S(1)}, bf16[128,384]{1,0:T(8,128)(2,1)S(1)}, u32[]{:S(2)}, u32[]{:S(2)}) collective-permute-start(bf16[128,384]{1,0:T(8,128)(2,1)S(1)} %totals.1.refs_0_), channel_id=1, source_target_pairs={{0,16},{4,20},{8,24},{12,28},{16,0},{20,4},{24,8},{28,12},{1,17},{... | collective-permute-start | bytes 294920 | tf_op jit(solution)/shard_map/ppermute | solution.py:679
  143.1 4.6 %collective-permute-start.9 = (bf16[128,384]{1,0:T(8,128)(2,1)S(1)}, bf16[128,384]{1,0:T(8,128)(2,1)S(1)}, u32[]{:S(2)}, u32[]{:S(2)}) collective-permute-start(bf16[128,384]{1,0:T(8,128)(2,1)S(1)} %totals.1.refs_0_), channel_id=1, source_target_pairs={{0,8},{4,12},{8,0},{12,4},{16,24},{20,28},{24,16},{28,20},{1,9},{5... | collective-permute-start | bytes 294920 | tf_op jit(solution)/shard_map/ppermute | solution.py:679
  143.7 4.0 %collective-permute-start.12 = (bf16[128,384]{1,0:T(8,128)(2,1)S(1)}, bf16[128,384]{1,0:T(8,128)(2,1)S(1)}, u32[]{:S(2)}, u32[]{:S(2)}) collective-permute-start(bf16[128,384]{1,0:T(8,128)(2,1)S(1)} %totals.1.refs_0_), channel_id=1, source_target_pairs={{0,4},{4,0},{8,12},{12,8},{16,20},{20,16},{24,28},{28,24},{1,5},{5... | collective-permute-start | bytes 294920 | tf_op jit(solution)/shard_map/ppermute | solution.py:679
  145.8 1.9 %collective-permute-start.15 = (bf16[128,384]{1,0:T(8,128)(2,1)S(1)}, bf16[128,384]{1,0:T(8,128)(2,1)S(1)}, u32[]{:S(2)}, u32[]{:S(2)}) collective-permute-start(bf16[128,384]{1,0:T(8,128)(2,1)S(1)} %collective-permute-done.11.refs_3_), channel_id=1, source_target_pairs={{0,4},{4,0},{8,12},{12,8},{16,20},{20,16},{24,28},{28,24},{1,5},{5... | collective-permute-start | bytes 294920 | tf_op jit(solution)/shard_map/ppermute | solution.py:679
  146.8 1.3 collective-permute-start.14
  147.7 1.3 collective-permute-start.13
Sparse Core Ops, SparseCore 0:
  85.7 42.3 reduce-scatter.1

commit v2 on v1

--- a/solution.py
+++ b/solution.py
@@ -441,14 +441,15 @@
         start_all(writes(last, set_a))
 
     chips, size = gw_ref.shape[1] // 2, gw_ref.shape[2]
+    ring = plane_ring(2 * chips)
     gw_copy = lambda s: pltpu.make_async_copy(gw_ref.at[s], gw_hbm.at[:, s], gw_sems.at[s])
     for s in range(blocks):
         cols = slice(s * D, (s + 1) * D)
         vec_ref[pl.ds(4 + (place ^ s), 1), :] = g1_ref[D : D + 1, cols]
         for i in range(chips):
             rows_of = slice(i * size, (i + 1) * size)
-            gw_ref[s, 2 * i] = g1_ref[rows_of, cols].astype(jnp.bfloat16)
-            gw_ref[s, 2 * i + 1] = g2_ref[rows_of, cols].astype(jnp.bfloat16)
+            gw_ref[s, ring.index(2 * i)] = g1_ref[rows_of, cols].astype(jnp.bfloat16)
+            gw_ref[s, ring.index(2 * i + 1)] = g2_ref[rows_of, cols].astype(jnp.bfloat16)
         gw_copy(s).start()
 
     sums = [jnp.sum(sum_ref[8 * i : 8 * i + 8, :], axis=0, keepdims=True) for i in range(6)]
@@ -520,11 +521,11 @@
     )(conv, image_rows, out_grad, moments, *vectors, *own, *direct, *other)
 
 
-def conv_back_kernel(
-    total, dbn_ref, conv_ref, grad_ref, image_ref, khat_ref, moments_ref, bn_sums_ref, vec_ref, bn_gain_ref,
-    forward_ref, inverse_ref, to_taps_ref,
-    in_grad_ref, taps_ref,
-    dconv_ref, image_grad_ref, product_ref, dhat_ref, all_taps_ref,
+def spectra_kernel(
+    total, dbn_ref, conv_ref, image_ref, khat_ref, moments_ref, bn_sums_ref, vec_ref, bn_gain_ref,
+    forward_ref, to_taps_ref,
+    product_ref, taps_ref,
+    dconv_ref, dhat_ref, all_taps_ref,
 ):
     step = pl.program_id(0)
     mean, bn_inv = batch_norm_terms(moments_ref, total)
@@ -560,9 +561,6 @@
                     tap_im.append(xr * gi - xi * gr)
             dhat_ref[re, :] += tree_sum(tap_re)
             dhat_ref[im, :] += tree_sum(tap_im)
-        for m in images:
-            put_pair(image_grad_ref, m, dot(inverse_ref[...], product_ref[m]))
-    in_grad_ref[...] = (image_grad_ref[...] + as_float(grad_ref[...])).astype(jnp.bfloat16)
 
     @pl.when(step == pl.num_programs(0) - 1)
     def _():
@@ -580,34 +578,58 @@
                 taps_ref[i] = jnp.zeros((size, D), jnp.bfloat16)
 
 
-def conv_backward(total, dbn, conv, out_grad, image_rows, khat, moments, bn_sums, vec, bn_gain, tables):
+def gradient_spectra(total, dbn, conv, image_rows, khat, moments, bn_sums, vec, bn_gain, tables):
     rows = conv.shape[0]
     steps = rows // STEP
-    forward, inverse, _, to_taps = tables
+    forward, _, _, to_taps = tables
     devices = lax.axis_size("dp") * lax.axis_size("mp")
     f32, bf16 = jnp.float32, jnp.bfloat16
     block = pl.BlockSpec((STEP, D), lambda i: (i, 0))
+    spectra = pl.BlockSpec((4, FROWS, 2 * D), lambda i: (i, 0, 0))
     taps = jax.ShapeDtypeStruct((devices, max(8, NTAPS // devices), D), bf16)
     return pl.pallas_call(
-        lambda *refs: conv_back_kernel(total, *refs),
+        lambda *refs: spectra_kernel(total, *refs),
         grid=(steps,),
-        in_specs=[block] * 4
-        + [whole(a) for a in (khat, moments, bn_sums, vec, bn_gain, forward, inverse, to_taps)],
-        out_specs=[block, whole(taps)],
-        out_shape=[jax.ShapeDtypeStruct((rows, D), bf16), taps],
+        in_specs=[block] * 3
+        + [whole(a) for a in (khat, moments, bn_sums, vec, bn_gain, forward, to_taps)],
+        out_specs=[spectra, whole(taps)],
+        out_shape=[jax.ShapeDtypeStruct((4 * steps, FROWS, 2 * D), bf16), taps],
         scratch_shapes=[
             pltpu.VMEM((STEP, D), bf16),
-            pltpu.VMEM((STEP, D), f32),
-            pltpu.VMEM((4, FROWS, 2 * D), bf16),
             pltpu.VMEM((FROWS, D), f32),
             pltpu.VMEM((NTAPS, D), f32),
         ],
         compiler_params=pltpu.CompilerParams(vmem_limit_bytes=VMEM_LIMIT),
         cost_estimate=pl.CostEstimate(
-            flops=4 * rows * D * FROWS, bytes_accessed=rows * D * 18, transcendentals=0
+            flops=2 * rows * D * FROWS, bytes_accessed=rows * D * 26, transcendentals=0
         ),
-        name="conv_backward",
-    )(dbn, conv, out_grad, image_rows, khat, moments, bn_sums, vec, bn_gain, forward, inverse, to_taps)
+        name="gradient_spectra",
+    )(dbn, conv, image_rows, khat, moments, bn_sums, vec, bn_gain, forward, to_taps)
+
+
+def inverse_kernel(product_ref, grad_ref, inverse_ref, in_grad_ref, image_grad_ref):
+    for m in range(4):
+        put_pair(image_grad_ref, m, dot(inverse_ref[...], product_ref[m]))
+    in_grad_ref[...] = (image_grad_ref[...] + as_float(grad_ref[...])).astype(jnp.bfloat16)
+
+
+def image_gradient(product, out_grad, tables):
+    rows = out_grad.shape[0]
+    inverse = tables[1]
+    block = pl.BlockSpec((STEP, D), lambda i: (i, 0))
+    return pl.pallas_call(
+        inverse_kernel,
+        grid=(rows // STEP,),
+        in_specs=[pl.BlockSpec((4, FROWS, 2 * D), lambda i: (i, 0, 0)), block, whole(inverse)],
+        out_specs=block,
+        out_shape=jax.ShapeDtypeStruct((rows, D), jnp.bfloat16),
+        scratch_shapes=[pltpu.VMEM((STEP, D), jnp.float32)],
+        compiler_params=pltpu.CompilerParams(vmem_limit_bytes=VMEM_LIMIT),
+        cost_estimate=pl.CostEstimate(
+            flops=2 * rows * D * FROWS, bytes_accessed=rows * D * 10, transcendentals=0
+        ),
+        name="image_gradient",
+    )(product, out_grad, inverse)
 
 
 def finish_kernel(chips, *refs):
@@ -708,8 +730,14 @@
     return [got[s] for s in range(1, lax.axis_size("mp"))]
 
 
+def plane_ring(size):
+    return [0, 1, 3, 2, 6, 7, 5, 4] if size == 8 else list(range(size))
+
+
 def reduce_weight_grads(parts):
-    return lax.optimization_barrier(lax.psum_scatter(parts, "dp", scatter_dimension=0, tiled=False))
+    groups = [plane_ring(lax.axis_size("dp"))]
+    mine = lax.psum_scatter(parts, "dp", scatter_dimension=0, axis_index_groups=groups, tiled=False)
+    return lax.optimization_barrier(mine)
 
 
 def message_kernel(taps_ref, weights_ref, own_ref, *message_refs):
@@ -738,7 +766,7 @@
         out_shape=[rows(size + count, jnp.float32)] + [rows(size + count, jnp.bfloat16)] * (places - 1),
         compiler_params=pltpu.CompilerParams(vmem_limit_bytes=SMALL_VMEM),
         name="messages",
-    )(exchange(taps), weights)
+    )(taps, weights)
     got = swap_places(messages)
     mine = pl.pallas_call(
         total_kernel,
@@ -777,7 +805,9 @@
     )
     bn_sums = exchange(bn_sums)
     weights = reduce_weight_grads(gw)
-    in_grad, taps = conv_backward(total, dbn, conv, out_grad, image_rows, khat, moments, bn_sums, vec, bn_gain, tables)
+    product, taps = gradient_spectra(total, dbn, conv, image_rows, khat, moments, bn_sums, vec, bn_gain, tables)
+    in_grad = image_gradient(product, out_grad, tables)
+    taps, in_grad = lax.optimization_barrier((exchange(taps), in_grad))
     mine, other = reduce_rest(taps, weights)
     tall_grad, wide_grad, small_grad, fc1_grad, fc2_grad, *vec = finish(mine, other, masks, bn_sums)
     tall_grad = turn(tall_grad)

time: 158 us -> 154 us (0.975)
  waiting for transfers between devices: 22.2 us -> 14.7 us
  Pallas kernels: 75.9 us -> 79.7 us
    reduce_scatter x1, waiting for transfers between devices: 8.25 us -> 0.01 us  [reduce_weight_grads(): lax.psum_scatter(parts, 'dp', scatter_dimension=0, axis_index_groups=grou...]
    pallas_call x1 -> x2, Pallas kernels: 20.1 us -> 24 us  [the longest x1 17.3 us: gradient_spectra(): pl.pallas_call(lambda *refs: spectra_kernel(total, *refs), grid=(steps,),...]
  transfers between devices with their start and end apart: 18 -> 18, of which waited for: 12 -> 11; matrix products, arithmetic and copies ran while one was open for 0% -> 0% of each run, Pallas kernels for 20% -> 23%
where the time goes in v2:
time: 154 us
  Pallas kernels  79.7 us (52%)
  blocking collectives  23.3 us (15%)
  starting transfers between devices  18.4 us (12%)
  waiting for transfers between devices  14.7 us (10%)
  between operations  14.2 us (9%)
  local copies, waits for them, and re-layouts  2.54 us (2%)
    pallas_call x1, Pallas kernels, mlp(): pl.pallas_call(lambda *refs: mlp_kernel(total, *refs), in_specs=[hbm] * 3...  42.4 us
    all_to_all x2, blocking collectives, exchange(): return lax.all_to_all(x, ('dp', 'mp'), split_axis=0, concat_axis=0)  23.3 us
    pallas_call x1, Pallas kernels, gradient_spectra(): pl.pallas_call(lambda *refs: spectra_kernel(total, *refs), grid=(steps,),...  17.3 us
    ppermute x16, starting transfers between devices, swap(): return lax.ppermute(x, axis, [(i, i ^ bit) for i in range(size)])  15.8 us
    ppermute x16, waiting for transfers between devices, swap(): return lax.ppermute(x, axis, [(i, i ^ bit) for i in range(size)])  12.1 us
    pallas_call x1, Pallas kernels, conv_forward(): pl.pallas_call(conv_kernel, grid=(steps,), in_specs=[pl.BlockSpec((STEP,...  11.5 us
    pallas_call x1, Pallas kernels, image_gradient(): pl.pallas_call(inverse_kernel, grid=(rows // STEP,), in_specs=[pl.BlockSp...  6.68 us
  transfers between devices with their start and end apart: 18, of which 11 were waited for; matrix products, arithmetic and copies ran while one was open for 0% of the time, Pallas kernels for 23%

profile of v2, /device:TPU:0, one launch (start us, length us, event | category | flops | bytes accessed | tf_op | source)
XLA Modules:
  0.0 153.9 jit_solution(1089713521391010744)
XLA Ops:
  7.2 0.0 reduce-scatter.2.cloned.1.call-start
  7.2 1.0 broadcast_select_fusion
  8.2 4.1 %collective-permute-start.1 = (bf16[384,384]{1,0:T(8,128)(2,1)S(1)}, bf16[384,384]{1,0:T(8,128)(2,1)S(1)}, u32[]{:S(2)}, u32[]{:S(2)}) collective-permute-start(bf16[384,384]{1,0:T(8,128)(2,1)S(1)} %broadcast_select_fusion), channel_id=1, source_target_pairs={{0,2},{1,3},{2,0},{3,1},{4,6},{5,7},{6,4},{7,5},{8,10},{9,11},{10,... | collective-permute-start | bytes 884744 | tf_op jit(solution)/shard_map/ppermute | solution.py:701
  12.3 1.6 %collective-permute-start = (bf16[384,384]{1,0:T(8,128)(2,1)S(1)}, bf16[384,384]{1,0:T(8,128)(2,1)S(1)}, u32[]{:S(2)}, u32[]{:S(2)}) collective-permute-start(bf16[384,384]{1,0:T(8,128)(2,1)S(1)} %broadcast_select_fusion), channel_id=1, source_target_pairs={{0,1},{1,0},{2,3},{3,2},{4,5},{5,4},{6,7},{7,6},{8,9},{9,8},{10,11... | collective-permute-start | bytes 884744 | tf_op jit(solution)/shard_map/ppermute | solution.py:701
  13.9 11.5 %conv_forward.1 = (f32[3136,384]{1,0:T(8,128)}, f32[736,384]{1,0:T(8,128)}, f32[32,2,384]{2,1,0:T(2,128)}) custom-call(bf16[3136,384]{1,0:T(8,128)(2,1)} %refs_2_.3, f32[5,51,384]{2,1,0:T(8,128)} %bitcast.7, f32[5,51,384]{2,1,0:T(8,128)} %wide_ref.1, f32[5,5,384]{2,1,0:T(8,128)} %small_ref.1, s32[5,51,384]{2,1,0:T(8,128)} %bitcast.4, s32[5,51,384]{2,1,0:T(8,128)} %refs_9_.4, ...), custom_call_target="tpu_custom_call" | custom-call | flops 3545235456 | bytes 12042240 | tf_op jit(solution)/shard_map/conv_forward/pallas_call | solution.py:194
  25.5 0.3 collective-permute-done.1.refs_14_
  25.8 0.2 collective-permute-done.refs_13_
  26.0 0.0 collective-permute-start.3
  26.0 0.5 collective-permute-start.4
  26.5 1.5 collective-permute-start.2
  28.0 12.7 %all_to_all.15.refs_3_.refs_4_ = f32[32,2,384]{2,1,0:T(2,128)} all-to-all(f32[32,2,384]{2,1,0:T(2,128)} %get-tuple-element.52), channel_id=1, replica_groups=mesh['dp'=8,'mp'=4] {'dp','mp'}, dimensions={0} | all-to-all | bytes 196608 | tf_op jit(solution)/shard_map/all_to_all | solution.py:231
  40.7 0.0 collective-permute-done.4.refs_17_
  40.7 0.0 copy-start.10
  40.7 0.1 collective-permute-start.5
  40.8 1.6 %collective-permute-done.5.refs_18_ = bf16[384,384]{1,0:T(8,128)(2,1)S(1)} collective-permute-done((bf16[384,384]{1,0:T(8,128)(2,1)S(1)}, bf16[384,384]{1,0:T(8,128)(2,1)S(1)}, u32[]{:S(2)}, u32[]{:S(2)}) %collective-permute-start.5) | collective-permute-done | bytes 294944 | tf_op jit(solution)/shard_map/ppermute | solution.py:701
  42.4 0.7 copy-done.11
  43.1 42.4 %mlp.1 = (bf16[3136,384]{1,0:T(8,128)(2,1)}, f32[3136,384]{1,0:T(8,128)}, bf16[8,4,96,384]{3,2,1,0:T(8,128)(2,1)}, f32[32,2,384]{2,1,0:T(2,128)}, f32[8,384]{1,0:T(8,128)}) custom-call(f32[3136,384]{1,0:T(8,128)} %get-tuple-element.51.refs_0_.refs_1_, bf16[3136,384]{1,0:T(8,128)(2,1)} %refs_2_.3, bf16[3136,384]{1,0:T(8,128)(2,1)} %grad_ref.1, ...), custom_call_target="tpu_custom_call" | custom-call | flops 22196256768 | bytes 24084480 | tf_op jit(solution)/shard_map/mlp/pallas_call | solution.py:473
  85.5 0.0 reduce-scatter.2.cloned.1.call-update
  85.5 0.9 copy-done.5
  86.4 10.6 %all_to_all.16.refs_5_.refs_11_ = f32[32,2,384]{2,1,0:T(2,128)} all-to-all(f32[32,2,384]{2,1,0:T(2,128)S(1)} %copy-done.5), channel_id=1, replica_groups=mesh['dp'=8,'mp'=4] {'dp','mp'}, dimensions={0} | all-to-all | bytes 196608 | tf_op jit(solution)/shard_map/all_to_all | solution.py:231
  97.0 17.3 %gradient_spectra.1 = (bf16[8,736,768]{2,1,0:T(8,128)(2,1)}, bf16[32,8,384]{2,1,0:T(8,128)(2,1)}) custom-call(f32[3136,384]{1,0:T(8,128)} %get-tuple-element.63.refs_0_, f32[3136,384]{1,0:T(8,128)} %get-tuple-element.51.refs_0_.refs_1_, bf16[3136,384]{1,0:T(8,128)(2,1)} %refs_2_.3, f32[736,384]{1,0:T(8,128)} %get-tuple-element.64.refs_3_, ...), custom_call_target="tpu_custom_call" | custom-call | flops 1772617728 | bytes 31309824 | tf_op jit(solution)/shard_map/gradient_spectra/pallas_call | solution.py:590
  114.4 2.6 %all-to-all-start.2 = ((bf16[32,8,384]{2,1,0:T(8,128)(2,1)}), bf16[32,8,384]{2,1,0:T(8,128)(2,1)S(1)}, u32[]{:S(2)}, u32[]{:S(2)}) async-start(bf16[32,8,384]{2,1,0:T(8,128)(2,1)} %get-tuple-element.67), calls=%async_computation.2 | async-start | bytes 393216 | tf_op jit(solution)/shard_map/all_to_all | solution.py:231
  117.0 0.0 copy-start.1
  117.0 0.0 copy-start.2
  117.0 0.0 copy-start.4
  117.0 6.7 %image_gradient.1 = bf16[3136,384]{1,0:T(8,128)(2,1)} custom-call(bf16[8,736,768]{2,1,0:T(8,128)(2,1)} %get-tuple-element.68.product_ref, bf16[3136,384]{1,0:T(8,128)(2,1)} %grad_ref.1, bf16[196,736]{1,0:T(8,128)(2,1)} %constant.29.clone.inverse_ref), custom_call_target="tpu_custom_call" | custom-call | flops 1772617728 | bytes 12042240 | tf_op jit(solution)/shard_map/image_gradient/pallas_call | solution.py:620
  123.7 2.6 %all-to-all-done.2.taps_ref = bf16[32,8,384]{2,1,0:T(8,128)(2,1)S(1)} async-done(((bf16[32,8,384]{2,1,0:T(8,128)(2,1)}), bf16[32,8,384]{2,1,0:T(8,128)(2,1)S(1)}, u32[]{:S(2)}, u32[]{:S(2)}) %all-to-all-start.2) | async-done | bytes 196640 | tf_op jit(solution)/shard_map/all_to_all | solution.py:231
  126.3 1.0 copy-done.3
  127.3 0.1 messages.1
  127.3 0.1 collective-permute-start.6
  127.4 2.0 %collective-permute-start.7 = (bf16[104,384]{1,0:T(8,128)(2,1)S(1)}, bf16[104,384]{1,0:T(8,128)(2,1)S(1)}, u32[]{:S(2)}, u32[]{:S(2)}) collective-permute-start(bf16[104,384]{1,0:T(8,128)(2,1)S(1)} %get-tuple-element.74), channel_id=1, source_target_pairs={{0,2},{1,3},{2,0},{3,1},{4,6},{5,7},{6,4},{7,5},{8,10},{9,11},{10,... | collective-permute-start | bytes 239624 | tf_op jit(solution)/shard_map/ppermute | solution.py:701
  129.3 2.4 %collective-permute-start.8 = (bf16[104,384]{1,0:T(8,128)(2,1)S(1)}, bf16[104,384]{1,0:T(8,128)(2,1)S(1)}, u32[]{:S(2)}, u32[]{:S(2)}) collective-permute-start(bf16[104,384]{1,0:T(8,128)(2,1)S(1)} %get-tuple-element.75), channel_id=1, source_target_pairs={{0,3},{1,2},{2,1},{3,0},{4,7},{5,6},{6,5},{7,4},{8,11},{9,10},{10,... | collective-permute-start | bytes 239624 | tf_op jit(solution)/shard_map/ppermute | solution.py:701
  131.8 0.9 collective-permute-done.6.refs_0_
  132.7 4.2 %collective-permute-done.7.refs_1_ = bf16[104,384]{1,0:T(8,128)(2,1)S(1)} collective-permute-done((bf16[104,384]{1,0:T(8,128)(2,1)S(1)}, bf16[104,384]{1,0:T(8,128)(2,1)S(1)}, u32[]{:S(2)}, u32[]{:S(2)}) %collective-permute-start.7) | collective-permute-done | bytes 79904 | tf_op jit(solution)/shard_map/ppermute | solution.py:701
  136.9 1.4 collective-permute-start.11
  138.4 1.2 collective-permute-start.10
  139.5 1.0 collective-permute-start.9
  140.5 0.0 collective-permute-start.12
  140.5 2.1 %collective-permute-done.11.refs_3_ = bf16[128,384]{1,0:T(8,128)(2,1)S(1)} collective-permute-done((bf16[128,384]{1,0:T(8,128)(2,1)S(1)}, bf16[128,384]{1,0:T(8,128)(2,1)S(1)}, u32[]{:S(2)}, u32[]{:S(2)}) %collective-permute-start.11) | collective-permute-done | bytes 98336 | tf_op jit(solution)/shard_map/ppermute | solution.py:701
  142.6 0.0 collective-permute-start.15
  142.6 1.0 collective-permute-done.10.refs_2_
  143.6 0.0 collective-permute-start.14
  143.6 0.6 collective-permute-done.9.refs_1_
  144.1 0.0 collective-permute-done.12.refs_4_
  144.1 0.0 collective-permute-done.15.refs_7_
  144.1 0.7 collective-permute-done.14.refs_6_
  144.9 0.6 collective-permute-done.13.refs_5_
  145.4 1.6 %finish.1 = (f32[5,51,384]{2,1,0:T(8,128)}, f32[5,51,384]{2,1,0:T(8,128)}, f32[5,5,384]{2,1,0:T(8,128)}, f32[384,384]{1,0:T(8,128)}, f32[384,384]{1,0:T(8,128)},...) custom-call(bf16[128,384]{1,0:T(8,128)(2,1)S(1)} %totals.1.refs_0_, ...), custom_call_target="tpu_custom_call" | custom-call | tf_op jit(solution)/shard_map/finish/pallas_call | solution.py:687
  (23 shorter events, 0.1 us)
Async XLA Ops:
  7.2 119.1 %reduce-scatter.2.cloned.1.call-start = ((), (), s32[]{:S(2)}) async-start(), calls=%async_computation.4 | async-start | bytes 2654208 | tf_op jit(solution)/shard_map/reduce_scatter | solution.py:739
  8.2 17.5 %collective-permute-start.1 = (bf16[384,384]{1,0:T(8,128)(2,1)S(1)}, bf16[384,384]{1,0:T(8,128)(2,1)S(1)}, u32[]{:S(2)}, u32[]{:S(2)}) collective-permute-start(bf16[384,384]{1,0:T(8,128)(2,1)S(1)} %broadcast_select_fusion), channel_id=1, source_target_pairs={{0,2},{1,3},{2,0},{3,1},{4,6},{5,7},{6,4},{7,5},{8,10},{9,11},{10,... | collective-permute-start | bytes 884744 | tf_op jit(solution)/shard_map/ppermute | solution.py:701
  12.3 13.6 %collective-permute-start = (bf16[384,384]{1,0:T(8,128)(2,1)S(1)}, bf16[384,384]{1,0:T(8,128)(2,1)S(1)}, u32[]{:S(2)}, u32[]{:S(2)}) collective-permute-start(bf16[384,384]{1,0:T(8,128)(2,1)S(1)} %broadcast_select_fusion), channel_id=1, source_target_pairs={{0,1},{1,0},{2,3},{3,2},{4,5},{5,4},{6,7},{7,6},{8,9},{9,8},{10,11... | collective-permute-start | bytes 884744 | tf_op jit(solution)/shard_map/ppermute | solution.py:701
  25.8 16.6 %copy-start.6 = (bf16[384,384]{1,0:T(8,128)(2,1)}, bf16[384,384]{1,0:T(8,128)(2,1)S(1)}, u32[]{:S(2)}) copy-start(bf16[384,384]{1,0:T(8,128)(2,1)S(1)} %collective-permute-done.1.refs_14_) | copy-start | bytes 884740
  26.0 16.4 %copy-start.7 = (bf16[384,384]{1,0:T(8,128)(2,1)}, bf16[384,384]{1,0:T(8,128)(2,1)S(1)}, u32[]{:S(2)}) copy-start(bf16[384,384]{1,0:T(8,128)(2,1)S(1)} %collective-permute-done.refs_13_) | copy-start | bytes 884740
  26.0 14.7 %collective-permute-start.3 = (bf16[384,384]{1,0:T(8,128)(2,1)S(1)}, bf16[384,384]{1,0:T(8,128)(2,1)S(1)}, u32[]{:S(2)}, u32[]{:S(2)}) collective-permute-start(bf16[384,384]{1,0:T(8,128)(2,1)S(1)} %collective-permute-done.refs_13_), channel_id=1, source_target_pairs={{0,4},{4,0},{8,12},{12,8},{16,20},{20,16},{24,28},{28,24},{1,5},{5... | collective-permute-start | bytes 884744 | tf_op jit(solution)/shard_map/ppermute | solution.py:701
  26.0 14.7 %collective-permute-start.4 = (bf16[384,384]{1,0:T(8,128)(2,1)S(1)}, bf16[384,384]{1,0:T(8,128)(2,1)S(1)}, u32[]{:S(2)}, u32[]{:S(2)}) collective-permute-start(bf16[384,384]{1,0:T(8,128)(2,1)S(1)} %collective-permute-done.1.refs_14_), channel_id=1, source_target_pairs={{0,4},{4,0},{8,12},{12,8},{16,20},{20,16},{24,28},{28,24},{1,5},{5... | collective-permute-start | bytes 884744 | tf_op jit(solution)/shard_map/ppermute | solution.py:701
  26.5 14.2 %collective-permute-start.2 = (bf16[384,384]{1,0:T(8,128)(2,1)S(1)}, bf16[384,384]{1,0:T(8,128)(2,1)S(1)}, u32[]{:S(2)}, u32[]{:S(2)}) collective-permute-start(bf16[384,384]{1,0:T(8,128)(2,1)S(1)} %collective-permute-done.1.refs_14_), channel_id=1, source_target_pairs={{0,1},{1,0},{2,3},{3,2},{4,5},{5,4},{6,7},{7,6},{8,9},{9,8},{10,11... | collective-permute-start | bytes 884744 | tf_op jit(solution)/shard_map/ppermute | solution.py:701
  40.7 1.7 %copy-start.8 = (bf16[384,384]{1,0:T(8,128)(2,1)}, bf16[384,384]{1,0:T(8,128)(2,1)S(1)}, u32[]{:S(2)}) copy-start(bf16[384,384]{1,0:T(8,128)(2,1)S(1)} %collective-permute-done.3.refs_16_) | copy-start | bytes 884740
  40.7 1.7 %copy-start.9 = (bf16[384,384]{1,0:T(8,128)(2,1)}, bf16[384,384]{1,0:T(8,128)(2,1)S(1)}, u32[]{:S(2)}) copy-start(bf16[384,384]{1,0:T(8,128)(2,1)S(1)} %collective-permute-done.4.refs_17_) | copy-start | bytes 884740
  40.7 1.7 %copy-start.10 = (bf16[384,384]{1,0:T(8,128)(2,1)}, bf16[384,384]{1,0:T(8,128)(2,1)S(1)}, u32[]{:S(2)}) copy-start(bf16[384,384]{1,0:T(8,128)(2,1)S(1)} %collective-permute-done.2.refs_15_) | copy-start | bytes 884740
  40.7 1.6 %collective-permute-start.5 = (bf16[384,384]{1,0:T(8,128)(2,1)S(1)}, bf16[384,384]{1,0:T(8,128)(2,1)S(1)}, u32[]{:S(2)}, u32[]{:S(2)}) collective-permute-start(bf16[384,384]{1,0:T(8,128)(2,1)S(1)} %collective-permute-done.2.refs_15_), channel_id=1, source_target_pairs={{0,4},{4,0},{8,12},{12,8},{16,20},{20,16},{24,28},{28,24},{1,5},{5... | collective-permute-start | bytes 884744 | tf_op jit(solution)/shard_map/ppermute | solution.py:701
  42.4 0.7 copy-start.11
  85.5 0.9 copy-start.5
  114.4 11.9 %all-to-all-start.2 = ((bf16[32,8,384]{2,1,0:T(8,128)(2,1)}), bf16[32,8,384]{2,1,0:T(8,128)(2,1)S(1)}, u32[]{:S(2)}, u32[]{:S(2)}) async-start(bf16[32,8,384]{2,1,0:T(8,128)(2,1)} %get-tuple-element.67), calls=%async_computation.2 | async-start | bytes 393216 | tf_op jit(solution)/shard_map/all_to_all | solution.py:231
  117.0 28.5 %copy-start = (f32[32,2,384]{2,1,0:T(2,128)S(1)}, f32[32,2,384]{2,1,0:T(2,128)}, u32[]{:S(2)}) copy-start(f32[32,2,384]{2,1,0:T(2,128)} %all_to_all.16.refs_5_.refs_11_) | copy-start | bytes 294916
  117.0 28.5 %copy-start.1 = (s32[51,5,384]{2,0,1:T(8,128)S(1)}, s32[51,5,384]{2,0,1:T(8,128)}, u32[]{:S(2)}) copy-start(s32[51,5,384]{2,0,1:T(8,128)} %param.25) | copy-start | bytes 1175044
  117.0 28.5 %copy-start.2 = (s32[5,51,384]{2,1,0:T(8,128)S(1)}, s32[5,51,384]{2,1,0:T(8,128)}, u32[]{:S(2)}) copy-start(s32[5,51,384]{2,1,0:T(8,128)} %refs_9_.4) | copy-start | bytes 1175044
  117.0 28.4 %copy-start.4 = (s32[5,5,384]{2,1,0:T(8,128)S(1)}, s32[5,5,384]{2,1,0:T(8,128)}, u32[]{:S(2)}) copy-start(s32[5,5,384]{2,1,0:T(8,128)} %refs_10_.3) | copy-start | bytes 115204
  126.3 1.0 copy-start.3
  127.3 5.4 %collective-permute-start.6 = (bf16[104,384]{1,0:T(8,128)(2,1)S(1)}, bf16[104,384]{1,0:T(8,128)(2,1)S(1)}, u32[]{:S(2)}, u32[]{:S(2)}) collective-permute-start(bf16[104,384]{1,0:T(8,128)(2,1)S(1)} %get-tuple-element.73), channel_id=1, source_target_pairs={{0,1},{1,0},{2,3},{3,2},{4,5},{5,4},{6,7},{7,6},{8,9},{9,8},{10,11... | collective-permute-start | bytes 239624 | tf_op jit(solution)/shard_map/ppermute | solution.py:701
  127.4 9.5 %collective-permute-start.7 = (bf16[104,384]{1,0:T(8,128)(2,1)S(1)}, bf16[104,384]{1,0:T(8,128)(2,1)S(1)}, u32[]{:S(2)}, u32[]{:S(2)}) collective-permute-start(bf16[104,384]{1,0:T(8,128)(2,1)S(1)} %get-tuple-element.74), channel_id=1, source_target_pairs={{0,2},{1,3},{2,0},{3,1},{4,6},{5,7},{6,4},{7,5},{8,10},{9,11},{10,... | collective-permute-start | bytes 239624 | tf_op jit(solution)/shard_map/ppermute | solution.py:701
  129.3 7.5 %collective-permute-start.8 = (bf16[104,384]{1,0:T(8,128)(2,1)S(1)}, bf16[104,384]{1,0:T(8,128)(2,1)S(1)}, u32[]{:S(2)}, u32[]{:S(2)}) collective-permute-start(bf16[104,384]{1,0:T(8,128)(2,1)S(1)} %get-tuple-element.75), channel_id=1, source_target_pairs={{0,3},{1,2},{2,1},{3,0},{4,7},{5,6},{6,5},{7,4},{8,11},{9,10},{10,... | collective-permute-start | bytes 239624 | tf_op jit(solution)/shard_map/ppermute | solution.py:701
  136.9 5.6 %collective-permute-start.11 = (bf16[128,384]{1,0:T(8,128)(2,1)S(1)}, bf16[128,384]{1,0:T(8,128)(2,1)S(1)}, u32[]{:S(2)}, u32[]{:S(2)}) collective-permute-start(bf16[128,384]{1,0:T(8,128)(2,1)S(1)} %totals.1.refs_0_), channel_id=1, source_target_pairs={{0,24},{4,28},{8,16},{12,20},{16,8},{20,12},{24,0},{28,4},{1,25},{... | collective-permute-start | bytes 294920 | tf_op jit(solution)/shard_map/ppermute | solution.py:701
  138.4 5.2 %collective-permute-start.10 = (bf16[128,384]{1,0:T(8,128)(2,1)S(1)}, bf16[128,384]{1,0:T(8,128)(2,1)S(1)}, u32[]{:S(2)}, u32[]{:S(2)}) collective-permute-start(bf16[128,384]{1,0:T(8,128)(2,1)S(1)} %totals.1.refs_0_), channel_id=1, source_target_pairs={{0,16},{4,20},{8,24},{12,28},{16,0},{20,4},{24,8},{28,12},{1,17},{... | collective-permute-start | bytes 294920 | tf_op jit(solution)/shard_map/ppermute | solution.py:701
  139.5 4.6 %collective-permute-start.9 = (bf16[128,384]{1,0:T(8,128)(2,1)S(1)}, bf16[128,384]{1,0:T(8,128)(2,1)S(1)}, u32[]{:S(2)}, u32[]{:S(2)}) collective-permute-start(bf16[128,384]{1,0:T(8,128)(2,1)S(1)} %totals.1.refs_0_), channel_id=1, source_target_pairs={{0,8},{4,12},{8,0},{12,4},{16,24},{20,28},{24,16},{28,20},{1,9},{5... | collective-permute-start | bytes 294920 | tf_op jit(solution)/shard_map/ppermute | solution.py:701
  140.5 3.6 %collective-permute-start.12 = (bf16[128,384]{1,0:T(8,128)(2,1)S(1)}, bf16[128,384]{1,0:T(8,128)(2,1)S(1)}, u32[]{:S(2)}, u32[]{:S(2)}) collective-permute-start(bf16[128,384]{1,0:T(8,128)(2,1)S(1)} %totals.1.refs_0_), channel_id=1, source_target_pairs={{0,4},{4,0},{8,12},{12,8},{16,20},{20,16},{24,28},{28,24},{1,5},{5... | collective-permute-start | bytes 294920 | tf_op jit(solution)/shard_map/ppermute | solution.py:701
  142.6 1.6 %collective-permute-start.15 = (bf16[128,384]{1,0:T(8,128)(2,1)S(1)}, bf16[128,384]{1,0:T(8,128)(2,1)S(1)}, u32[]{:S(2)}, u32[]{:S(2)}) collective-permute-start(bf16[128,384]{1,0:T(8,128)(2,1)S(1)} %collective-permute-done.11.refs_3_), channel_id=1, source_target_pairs={{0,4},{4,0},{8,12},{12,8},{16,20},{20,16},{24,28},{28,24},{1,5},{5... | collective-permute-start | bytes 294920 | tf_op jit(solution)/shard_map/ppermute | solution.py:701
  143.6 1.3 collective-permute-start.14
  144.1 1.3 collective-permute-start.13
Sparse Core Ops, SparseCore 0:
  85.7 28.5 reduce-scatter.1

commit v3 on v2

--- a/solution.py
+++ b/solution.py
@@ -373,7 +373,7 @@
         first = jnp.mean(d_hat, axis=1, keepdims=True)
         second = jnp.mean(d_hat * ln_hat, axis=1, keepdims=True)
         dbn = inv * (d_hat - first - ln_hat * second)
-        dbn_ref[at, :] = dbn
+        dbn_ref[at, :] = dbn.astype(jnp.bfloat16)
         sum_ref[0:8, :] += fold8(dbn * bn_hat)
         sum_ref[8:16, :] += fold8(dbn)
         sum_ref[16:24, :] += fold8(dnormed * ln_hat)
@@ -476,7 +476,7 @@
         out_specs=[hbm] * 3 + [vmem] * 2,
         out_shape=[
             jax.ShapeDtypeStruct((rows, D), bf16),
-            jax.ShapeDtypeStruct((rows, D), f32),
+            jax.ShapeDtypeStruct((rows, D), bf16),
             jax.ShapeDtypeStruct((2 * chips, blocks, D // chips, D), bf16),
             jax.ShapeDtypeStruct((2 * chips * blocks, 2, D), f32),
             jax.ShapeDtypeStruct((4 + blocks, D), f32),
@@ -491,7 +491,7 @@
             pltpu.VMEM((TILE, D), bf16),
             pltpu.VMEM((TILE, D), bf16),
             pltpu.VMEM((TILE, D), bf16),
-            pltpu.VMEM((TILE, D), f32),
+            pltpu.VMEM((TILE, D), bf16),
             pltpu.VMEM((TILE, D), bf16),
             pltpu.VMEM((TILE, D), bf16),
             pltpu.VMEM((D + 16, TILE), bf16),
@@ -540,7 +540,7 @@
     for r in range(0, STEP, LAST_ROWS):
         at = slice(r, r + LAST_ROWS)
         bn_hat = (conv_ref[at, :] - mean) * bn_inv
-        dconv = gain * (dbn_ref[at, :] - shift - bn_hat * slope)
+        dconv = gain * (as_float(dbn_ref[at, :]) - shift - bn_hat * slope)
         dconv_ref[at, :] = dconv.astype(jnp.bfloat16)
     for k in range(2):
         images = (2 * k, 2 * k + 1)
@@ -807,7 +807,7 @@
     weights = reduce_weight_grads(gw)
     product, taps = gradient_spectra(total, dbn, conv, image_rows, khat, moments, bn_sums, vec, bn_gain, tables)
     in_grad = image_gradient(product, out_grad, tables)
-    taps, in_grad = lax.optimization_barrier((exchange(taps), in_grad))
+    taps, in_grad, weights = lax.optimization_barrier((exchange(taps), in_grad, weights))
     mine, other = reduce_rest(taps, weights)
     tall_grad, wide_grad, small_grad, fc1_grad, fc2_grad, *vec = finish(mine, other, masks, bn_sums)
     tall_grad = turn(tall_grad)

time: 154 us -> 154 us (level)
  no operation moved by 1% of the time
where the time goes in v3:
time: 154 us
  Pallas kernels  79.7 us (52%)
  blocking collectives  23.4 us (15%)
  starting transfers between devices  18.4 us (12%)
  waiting for transfers between devices  14.6 us (9%)
  between operations  14.2 us (9%)
  local copies, waits for them, and re-layouts  2.54 us (2%)
    pallas_call x1, Pallas kernels, mlp(): pl.pallas_call(lambda *refs: mlp_kernel(total, *refs), in_specs=[hbm] * 3...  42.6 us
    all_to_all x2, blocking collectives, exchange(): return lax.all_to_all(x, ('dp', 'mp'), split_axis=0, concat_axis=0)  23.4 us
    pallas_call x1, Pallas kernels, gradient_spectra(): pl.pallas_call(lambda *refs: spectra_kernel(total, *refs), grid=(steps,),...  17.1 us
    ppermute x16, starting transfers between devices, swap(): return lax.ppermute(x, axis, [(i, i ^ bit) for i in range(size)])  15.8 us
    ppermute x16, waiting for transfers between devices, swap(): return lax.ppermute(x, axis, [(i, i ^ bit) for i in range(size)])  12 us
    pallas_call x1, Pallas kernels, conv_forward(): pl.pallas_call(conv_kernel, grid=(steps,), in_specs=[pl.BlockSpec((STEP,...  11.7 us
    pallas_call x1, Pallas kernels, image_gradient(): pl.pallas_call(inverse_kernel, grid=(rows // STEP,), in_specs=[pl.BlockSp...  6.68 us
  transfers between devices with their start and end apart: 18, of which 11 were waited for; matrix products, arithmetic and copies ran while one was open for 0% of the time, Pallas kernels for 23%

profile of v3, /device:TPU:0, one launch (start us, length us, event | category | flops | bytes accessed | tf_op | source)
XLA Modules:
  0.0 153.8 jit_solution(5646033642434960823)
XLA Ops:
  7.2 0.0 reduce-scatter.2.cloned.1.call-start
  7.2 1.0 broadcast_select_fusion
  8.2 4.1 %collective-permute-start.1 = (bf16[384,384]{1,0:T(8,128)(2,1)S(1)}, bf16[384,384]{1,0:T(8,128)(2,1)S(1)}, u32[]{:S(2)}, u32[]{:S(2)}) collective-permute-start(bf16[384,384]{1,0:T(8,128)(2,1)S(1)} %broadcast_select_fusion), channel_id=1, source_target_pairs={{0,2},{1,3},{2,0},{3,1},{4,6},{5,7},{6,4},{7,5},{8,10},{9,11},{10,... | collective-permute-start | bytes 884744 | tf_op jit(solution)/shard_map/ppermute | solution.py:701
  12.3 1.6 %collective-permute-start = (bf16[384,384]{1,0:T(8,128)(2,1)S(1)}, bf16[384,384]{1,0:T(8,128)(2,1)S(1)}, u32[]{:S(2)}, u32[]{:S(2)}) collective-permute-start(bf16[384,384]{1,0:T(8,128)(2,1)S(1)} %broadcast_select_fusion), channel_id=1, source_target_pairs={{0,1},{1,0},{2,3},{3,2},{4,5},{5,4},{6,7},{7,6},{8,9},{9,8},{10,11... | collective-permute-start | bytes 884744 | tf_op jit(solution)/shard_map/ppermute | solution.py:701
  13.9 11.7 %conv_forward.1 = (f32[3136,384]{1,0:T(8,128)}, f32[736,384]{1,0:T(8,128)}, f32[32,2,384]{2,1,0:T(2,128)}) custom-call(bf16[3136,384]{1,0:T(8,128)(2,1)} %refs_2_.3, f32[5,51,384]{2,1,0:T(8,128)} %bitcast.7, f32[5,51,384]{2,1,0:T(8,128)} %wide_ref.1, f32[5,5,384]{2,1,0:T(8,128)} %small_ref.1, s32[5,51,384]{2,1,0:T(8,128)} %bitcast.4, s32[5,51,384]{2,1,0:T(8,128)} %refs_9_.4, ...), custom_call_target="tpu_custom_call" | custom-call | flops 3545235456 | bytes 12042240 | tf_op jit(solution)/shard_map/conv_forward/pallas_call | solution.py:194
  25.6 0.2 collective-permute-done.1.refs_14_
  25.8 0.2 collective-permute-done.refs_13_
  26.0 0.0 collective-permute-start.3
  26.0 0.5 collective-permute-start.4
  26.5 1.5 collective-permute-start.2
  28.0 12.7 %all_to_all.15.refs_3_.refs_4_ = f32[32,2,384]{2,1,0:T(2,128)} all-to-all(f32[32,2,384]{2,1,0:T(2,128)} %get-tuple-element.53), channel_id=1, replica_groups=mesh['dp'=8,'mp'=4] {'dp','mp'}, dimensions={0} | all-to-all | bytes 196608 | tf_op jit(solution)/shard_map/all_to_all | solution.py:231
  40.7 0.0 collective-permute-done.3.refs_16_
  40.7 0.0 collective-permute-done.4.refs_17_
  40.7 0.0 collective-permute-done.2.refs_15_
  40.7 0.0 copy-start.10
  40.7 0.1 collective-permute-start.5
  40.8 1.6 %collective-permute-done.5.refs_18_ = bf16[384,384]{1,0:T(8,128)(2,1)S(1)} collective-permute-done((bf16[384,384]{1,0:T(8,128)(2,1)S(1)}, bf16[384,384]{1,0:T(8,128)(2,1)S(1)}, u32[]{:S(2)}, u32[]{:S(2)}) %collective-permute-start.5) | collective-permute-done | bytes 294944 | tf_op jit(solution)/shard_map/ppermute | solution.py:701
  42.4 0.7 copy-done.11
  43.1 42.6 %mlp.1 = (bf16[3136,384]{1,0:T(8,128)(2,1)}, bf16[3136,384]{1,0:T(8,128)(2,1)}, bf16[8,4,96,384]{3,2,1,0:T(8,128)(2,1)}, f32[32,2,384]{2,1,0:T(2,128)}, f32[8,384]{1,0:T(8,128)}) custom-call(f32[3136,384]{1,0:T(8,128)} %get-tuple-element.52.refs_0_.refs_1_, bf16[3136,384]{1,0:T(8,128)(2,1)} %refs_2_.3, bf16[3136,384]{1,0:T(8,128)(2,1)} %grad_ref.1, ...), custom_call_target="tpu_custom_call" | custom-call | flops 22196256768 | bytes 24084480 | tf_op jit(solution)/shard_map/mlp/pallas_call | solution.py:473
  85.7 0.0 reduce-scatter.2.cloned.1.call-update
  85.7 0.9 copy-done.5
  86.6 10.7 %all_to_all.16.refs_5_.refs_11_ = f32[32,2,384]{2,1,0:T(2,128)} all-to-all(f32[32,2,384]{2,1,0:T(2,128)S(1)} %copy-done.5), channel_id=1, replica_groups=mesh['dp'=8,'mp'=4] {'dp','mp'}, dimensions={0} | all-to-all | bytes 196608 | tf_op jit(solution)/shard_map/all_to_all | solution.py:231
  97.2 17.1 %gradient_spectra.1 = (bf16[8,736,768]{2,1,0:T(8,128)(2,1)}, bf16[32,8,384]{2,1,0:T(8,128)(2,1)}) custom-call(bf16[3136,384]{1,0:T(8,128)(2,1)} %get-tuple-element.64.refs_0_, f32[3136,384]{1,0:T(8,128)} %get-tuple-element.52.refs_0_.refs_1_, bf16[3136,384]{1,0:T(8,128)(2,1)} %refs_2_.3, f32[736,384]{1,0:T(8,128)} %get-tuple-element.65.refs_3_, ...), custom_call_target="tpu_custom_call" | custom-call | flops 1772617728 | bytes 31309824 | tf_op jit(solution)/shard_map/gradient_spectra/pallas_call | solution.py:590
  114.3 2.6 %all-to-all-start.2 = ((bf16[32,8,384]{2,1,0:T(8,128)(2,1)}), bf16[32,8,384]{2,1,0:T(8,128)(2,1)S(1)}, u32[]{:S(2)}, u32[]{:S(2)}) async-start(bf16[32,8,384]{2,1,0:T(8,128)(2,1)} %get-tuple-element.68), calls=%async_computation.2 | async-start | bytes 393216 | tf_op jit(solution)/shard_map/all_to_all | solution.py:231
  116.9 0.0 copy-start.1
  116.9 0.0 copy-start.2
  116.9 0.0 copy-start.4
  116.9 6.7 %image_gradient.1 = bf16[3136,384]{1,0:T(8,128)(2,1)} custom-call(bf16[8,736,768]{2,1,0:T(8,128)(2,1)} %get-tuple-element.69.product_ref, bf16[3136,384]{1,0:T(8,128)(2,1)} %grad_ref.1, bf16[196,736]{1,0:T(8,128)(2,1)} %constant.29.clone.inverse_ref), custom_call_target="tpu_custom_call" | custom-call | flops 1772617728 | bytes 12042240 | tf_op jit(solution)/shard_map/image_gradient/pallas_call | solution.py:620
  123.6 2.6 %all-to-all-done.2.taps_ref = bf16[32,8,384]{2,1,0:T(8,128)(2,1)S(1)} async-done(((bf16[32,8,384]{2,1,0:T(8,128)(2,1)}), bf16[32,8,384]{2,1,0:T(8,128)(2,1)S(1)}, u32[]{:S(2)}, u32[]{:S(2)}) %all-to-all-start.2) | async-done | bytes 196640 | tf_op jit(solution)/shard_map/all_to_all | solution.py:231
  126.2 1.0 copy-done.3
  127.2 0.1 messages.1
  127.2 0.1 collective-permute-start.6
  127.3 2.0 %collective-permute-start.7 = (bf16[104,384]{1,0:T(8,128)(2,1)S(1)}, bf16[104,384]{1,0:T(8,128)(2,1)S(1)}, u32[]{:S(2)}, u32[]{:S(2)}) collective-permute-start(bf16[104,384]{1,0:T(8,128)(2,1)S(1)} %get-tuple-element.76), channel_id=1, source_target_pairs={{0,2},{1,3},{2,0},{3,1},{4,6},{5,7},{6,4},{7,5},{8,10},{9,11},{10,... | collective-permute-start | bytes 239624 | tf_op jit(solution)/shard_map/ppermute | solution.py:701
  129.3 2.4 %collective-permute-start.8 = (bf16[104,384]{1,0:T(8,128)(2,1)S(1)}, bf16[104,384]{1,0:T(8,128)(2,1)S(1)}, u32[]{:S(2)}, u32[]{:S(2)}) collective-permute-start(bf16[104,384]{1,0:T(8,128)(2,1)S(1)} %get-tuple-element.77), channel_id=1, source_target_pairs={{0,3},{1,2},{2,1},{3,0},{4,7},{5,6},{6,5},{7,4},{8,11},{9,10},{10,... | collective-permute-start | bytes 239624 | tf_op jit(solution)/shard_map/ppermute | solution.py:701
  131.7 0.9 collective-permute-done.6.refs_0_
  132.6 4.2 %collective-permute-done.7.refs_1_ = bf16[104,384]{1,0:T(8,128)(2,1)S(1)} collective-permute-done((bf16[104,384]{1,0:T(8,128)(2,1)S(1)}, bf16[104,384]{1,0:T(8,128)(2,1)S(1)}, u32[]{:S(2)}, u32[]{:S(2)}) %collective-permute-start.7) | collective-permute-done | bytes 79904 | tf_op jit(solution)/shard_map/ppermute | solution.py:701
  136.8 0.0 collective-permute-done.8.refs_2_
  136.8 1.4 collective-permute-start.11
  138.3 1.2 collective-permute-start.10
  139.4 1.0 collective-permute-start.9
  140.4 2.1 %collective-permute-done.11.refs_3_ = bf16[128,384]{1,0:T(8,128)(2,1)S(1)} collective-permute-done((bf16[128,384]{1,0:T(8,128)(2,1)S(1)}, bf16[128,384]{1,0:T(8,128)(2,1)S(1)}, u32[]{:S(2)}, u32[]{:S(2)}) %collective-permute-start.11) | collective-permute-done | bytes 98336 | tf_op jit(solution)/shard_map/ppermute | solution.py:701
  142.5 1.0 collective-permute-done.10.refs_2_
  143.5 0.6 collective-permute-done.9.refs_1_
  144.0 0.0 collective-permute-start.13
  144.1 0.0 collective-permute-done.12.refs_4_
  144.1 0.7 collective-permute-done.14.refs_6_
  144.8 0.6 collective-permute-done.13.refs_5_
  145.4 1.6 %finish.1 = (f32[5,51,384]{2,1,0:T(8,128)}, f32[5,51,384]{2,1,0:T(8,128)}, f32[5,5,384]{2,1,0:T(8,128)}, f32[384,384]{1,0:T(8,128)}, f32[384,384]{1,0:T(8,128)},...) custom-call(bf16[128,384]{1,0:T(8,128)(2,1)S(1)} %totals.1.refs_0_, ...), custom_call_target="tpu_custom_call" | custom-call | tf_op jit(solution)/shard_map/finish/pallas_call | solution.py:687
  (23 shorter events, 0.1 us)
Async XLA Ops:
  7.2 116.4 %reduce-scatter.2.cloned.1.call-start = ((), (), s32[]{:S(2)}) async-start(), calls=%async_computation.4 | async-start | bytes 2654208 | tf_op jit(solution)/shard_map/reduce_scatter | solution.py:739
  8.2 17.5 %collective-permute-start.1 = (bf16[384,384]{1,0:T(8,128)(2,1)S(1)}, bf16[384,384]{1,0:T(8,128)(2,1)S(1)}, u32[]{:S(2)}, u32[]{:S(2)}) collective-permute-start(bf16[384,384]{1,0:T(8,128)(2,1)S(1)} %broadcast_select_fusion), channel_id=1, source_target_pairs={{0,2},{1,3},{2,0},{3,1},{4,6},{5,7},{6,4},{7,5},{8,10},{9,11},{10,... | collective-permute-start | bytes 884744 | tf_op jit(solution)/shard_map/ppermute | solution.py:701
  12.3 13.6 %collective-permute-start = (bf16[384,384]{1,0:T(8,128)(2,1)S(1)}, bf16[384,384]{1,0:T(8,128)(2,1)S(1)}, u32[]{:S(2)}, u32[]{:S(2)}) collective-permute-start(bf16[384,384]{1,0:T(8,128)(2,1)S(1)} %broadcast_select_fusion), channel_id=1, source_target_pairs={{0,1},{1,0},{2,3},{3,2},{4,5},{5,4},{6,7},{7,6},{8,9},{9,8},{10,11... | collective-permute-start | bytes 884744 | tf_op jit(solution)/shard_map/ppermute | solution.py:701
  25.8 16.6 %copy-start.6 = (bf16[384,384]{1,0:T(8,128)(2,1)}, bf16[384,384]{1,0:T(8,128)(2,1)S(1)}, u32[]{:S(2)}) copy-start(bf16[384,384]{1,0:T(8,128)(2,1)S(1)} %collective-permute-done.1.refs_14_) | copy-start | bytes 884740
  26.0 16.4 %copy-start.7 = (bf16[384,384]{1,0:T(8,128)(2,1)}, bf16[384,384]{1,0:T(8,128)(2,1)S(1)}, u32[]{:S(2)}) copy-start(bf16[384,384]{1,0:T(8,128)(2,1)S(1)} %collective-permute-done.refs_13_) | copy-start | bytes 884740
  26.0 14.7 %collective-permute-start.3 = (bf16[384,384]{1,0:T(8,128)(2,1)S(1)}, bf16[384,384]{1,0:T(8,128)(2,1)S(1)}, u32[]{:S(2)}, u32[]{:S(2)}) collective-permute-start(bf16[384,384]{1,0:T(8,128)(2,1)S(1)} %collective-permute-done.refs_13_), channel_id=1, source_target_pairs={{0,4},{4,0},{8,12},{12,8},{16,20},{20,16},{24,28},{28,24},{1,5},{5... | collective-permute-start | bytes 884744 | tf_op jit(solution)/shard_map/ppermute | solution.py:701
  26.0 14.7 %collective-permute-start.4 = (bf16[384,384]{1,0:T(8,128)(2,1)S(1)}, bf16[384,384]{1,0:T(8,128)(2,1)S(1)}, u32[]{:S(2)}, u32[]{:S(2)}) collective-permute-start(bf16[384,384]{1,0:T(8,128)(2,1)S(1)} %collective-permute-done.1.refs_14_), channel_id=1, source_target_pairs={{0,4},{4,0},{8,12},{12,8},{16,20},{20,16},{24,28},{28,24},{1,5},{5... | collective-permute-start | bytes 884744 | tf_op jit(solution)/shard_map/ppermute | solution.py:701
  26.5 14.2 %collective-permute-start.2 = (bf16[384,384]{1,0:T(8,128)(2,1)S(1)}, bf16[384,384]{1,0:T(8,128)(2,1)S(1)}, u32[]{:S(2)}, u32[]{:S(2)}) collective-permute-start(bf16[384,384]{1,0:T(8,128)(2,1)S(1)} %collective-permute-done.1.refs_14_), channel_id=1, source_target_pairs={{0,1},{1,0},{2,3},{3,2},{4,5},{5,4},{6,7},{7,6},{8,9},{9,8},{10,11... | collective-permute-start | bytes 884744 | tf_op jit(solution)/shard_map/ppermute | solution.py:701
  40.7 1.7 %copy-start.8 = (bf16[384,384]{1,0:T(8,128)(2,1)}, bf16[384,384]{1,0:T(8,128)(2,1)S(1)}, u32[]{:S(2)}) copy-start(bf16[384,384]{1,0:T(8,128)(2,1)S(1)} %collective-permute-done.3.refs_16_) | copy-start | bytes 884740
  40.7 1.7 %copy-start.9 = (bf16[384,384]{1,0:T(8,128)(2,1)}, bf16[384,384]{1,0:T(8,128)(2,1)S(1)}, u32[]{:S(2)}) copy-start(bf16[384,384]{1,0:T(8,128)(2,1)S(1)} %collective-permute-done.4.refs_17_) | copy-start | bytes 884740
  40.7 1.7 %copy-start.10 = (bf16[384,384]{1,0:T(8,128)(2,1)}, bf16[384,384]{1,0:T(8,128)(2,1)S(1)}, u32[]{:S(2)}) copy-start(bf16[384,384]{1,0:T(8,128)(2,1)S(1)} %collective-permute-done.2.refs_15_) | copy-start | bytes 884740
  40.7 1.6 %collective-permute-start.5 = (bf16[384,384]{1,0:T(8,128)(2,1)S(1)}, bf16[384,384]{1,0:T(8,128)(2,1)S(1)}, u32[]{:S(2)}, u32[]{:S(2)}) collective-permute-start(bf16[384,384]{1,0:T(8,128)(2,1)S(1)} %collective-permute-done.2.refs_15_), channel_id=1, source_target_pairs={{0,4},{4,0},{8,12},{12,8},{16,20},{20,16},{24,28},{28,24},{1,5},{5... | collective-permute-start | bytes 884744 | tf_op jit(solution)/shard_map/ppermute | solution.py:701
  42.4 0.7 copy-start.11
  85.7 0.9 copy-start.5
  114.3 11.9 %all-to-all-start.2 = ((bf16[32,8,384]{2,1,0:T(8,128)(2,1)}), bf16[32,8,384]{2,1,0:T(8,128)(2,1)S(1)}, u32[]{:S(2)}, u32[]{:S(2)}) async-start(bf16[32,8,384]{2,1,0:T(8,128)(2,1)} %get-tuple-element.68), calls=%async_computation.2 | async-start | bytes 393216 | tf_op jit(solution)/shard_map/all_to_all | solution.py:231
  116.9 28.5 %copy-start = (f32[32,2,384]{2,1,0:T(2,128)S(1)}, f32[32,2,384]{2,1,0:T(2,128)}, u32[]{:S(2)}) copy-start(f32[32,2,384]{2,1,0:T(2,128)} %all_to_all.16.refs_5_.refs_11_) | copy-start | bytes 294916
  116.9 28.5 %copy-start.1 = (s32[51,5,384]{2,0,1:T(8,128)S(1)}, s32[51,5,384]{2,0,1:T(8,128)}, u32[]{:S(2)}) copy-start(s32[51,5,384]{2,0,1:T(8,128)} %param.25) | copy-start | bytes 1175044
  116.9 28.4 %copy-start.2 = (s32[5,51,384]{2,1,0:T(8,128)S(1)}, s32[5,51,384]{2,1,0:T(8,128)}, u32[]{:S(2)}) copy-start(s32[5,51,384]{2,1,0:T(8,128)} %refs_9_.4) | copy-start | bytes 1175044
  116.9 28.4 %copy-start.4 = (s32[5,5,384]{2,1,0:T(8,128)S(1)}, s32[5,5,384]{2,1,0:T(8,128)}, u32[]{:S(2)}) copy-start(s32[5,5,384]{2,1,0:T(8,128)} %refs_10_.3) | copy-start | bytes 115204
  126.2 1.0 copy-start.3
  127.2 5.4 %collective-permute-start.6 = (bf16[104,384]{1,0:T(8,128)(2,1)S(1)}, bf16[104,384]{1,0:T(8,128)(2,1)S(1)}, u32[]{:S(2)}, u32[]{:S(2)}) collective-permute-start(bf16[104,384]{1,0:T(8,128)(2,1)S(1)} %get-tuple-element.75), channel_id=1, source_target_pairs={{0,1},{1,0},{2,3},{3,2},{4,5},{5,4},{6,7},{7,6},{8,9},{9,8},{10,11... | collective-permute-start | bytes 239624 | tf_op jit(solution)/shard_map/ppermute | solution.py:701
  127.3 9.5 %collective-permute-start.7 = (bf16[104,384]{1,0:T(8,128)(2,1)S(1)}, bf16[104,384]{1,0:T(8,128)(2,1)S(1)}, u32[]{:S(2)}, u32[]{:S(2)}) collective-permute-start(bf16[104,384]{1,0:T(8,128)(2,1)S(1)} %get-tuple-element.76), channel_id=1, source_target_pairs={{0,2},{1,3},{2,0},{3,1},{4,6},{5,7},{6,4},{7,5},{8,10},{9,11},{10,... | collective-permute-start | bytes 239624 | tf_op jit(solution)/shard_map/ppermute | solution.py:701
  129.3 7.5 %collective-permute-start.8 = (bf16[104,384]{1,0:T(8,128)(2,1)S(1)}, bf16[104,384]{1,0:T(8,128)(2,1)S(1)}, u32[]{:S(2)}, u32[]{:S(2)}) collective-permute-start(bf16[104,384]{1,0:T(8,128)(2,1)S(1)} %get-tuple-element.77), channel_id=1, source_target_pairs={{0,3},{1,2},{2,1},{3,0},{4,7},{5,6},{6,5},{7,4},{8,11},{9,10},{10,... | collective-permute-start | bytes 239624 | tf_op jit(solution)/shard_map/ppermute | solution.py:701
  136.8 5.6 %collective-permute-start.11 = (bf16[128,384]{1,0:T(8,128)(2,1)S(1)}, bf16[128,384]{1,0:T(8,128)(2,1)S(1)}, u32[]{:S(2)}, u32[]{:S(2)}) collective-permute-start(bf16[128,384]{1,0:T(8,128)(2,1)S(1)} %totals.1.refs_0_), channel_id=1, source_target_pairs={{0,24},{4,28},{8,16},{12,20},{16,8},{20,12},{24,0},{28,4},{1,25},{... | collective-permute-start | bytes 294920 | tf_op jit(solution)/shard_map/ppermute | solution.py:701
  138.3 5.2 %collective-permute-start.10 = (bf16[128,384]{1,0:T(8,128)(2,1)S(1)}, bf16[128,384]{1,0:T(8,128)(2,1)S(1)}, u32[]{:S(2)}, u32[]{:S(2)}) collective-permute-start(bf16[128,384]{1,0:T(8,128)(2,1)S(1)} %totals.1.refs_0_), channel_id=1, source_target_pairs={{0,16},{4,20},{8,24},{12,28},{16,0},{20,4},{24,8},{28,12},{1,17},{... | collective-permute-start | bytes 294920 | tf_op jit(solution)/shard_map/ppermute | solution.py:701
  139.4 4.6 %collective-permute-start.9 = (bf16[128,384]{1,0:T(8,128)(2,1)S(1)}, bf16[128,384]{1,0:T(8,128)(2,1)S(1)}, u32[]{:S(2)}, u32[]{:S(2)}) collective-permute-start(bf16[128,384]{1,0:T(8,128)(2,1)S(1)} %totals.1.refs_0_), channel_id=1, source_target_pairs={{0,8},{4,12},{8,0},{12,4},{16,24},{20,28},{24,16},{28,20},{1,9},{5... | collective-permute-start | bytes 294920 | tf_op jit(solution)/shard_map/ppermute | solution.py:701
  140.4 3.6 %collective-permute-start.12 = (bf16[128,384]{1,0:T(8,128)(2,1)S(1)}, bf16[128,384]{1,0:T(8,128)(2,1)S(1)}, u32[]{:S(2)}, u32[]{:S(2)}) collective-permute-start(bf16[128,384]{1,0:T(8,128)(2,1)S(1)} %totals.1.refs_0_), channel_id=1, source_target_pairs={{0,4},{4,0},{8,12},{12,8},{16,20},{20,16},{24,28},{28,24},{1,5},{5... | collective-permute-start | bytes 294920 | tf_op jit(solution)/shard_map/ppermute | solution.py:701
  142.5 1.6 %collective-permute-start.15 = (bf16[128,384]{1,0:T(8,128)(2,1)S(1)}, bf16[128,384]{1,0:T(8,128)(2,1)S(1)}, u32[]{:S(2)}, u32[]{:S(2)}) collective-permute-start(bf16[128,384]{1,0:T(8,128)(2,1)S(1)} %collective-permute-done.11.refs_3_), channel_id=1, source_target_pairs={{0,4},{4,0},{8,12},{12,8},{16,20},{20,16},{24,28},{28,24},{1,5},{5... | collective-permute-start | bytes 294920 | tf_op jit(solution)/shard_map/ppermute | solution.py:701
  143.5 1.3 collective-permute-start.14
  144.0 1.3 collective-permute-start.13
Sparse Core Ops, SparseCore 0:
  85.8 28.6 reduce-scatter.1

commit v4 on v2

--- a/solution.py
+++ b/solution.py
@@ -524,10 +524,18 @@
 def spectra_kernel(
     total, dbn_ref, conv_ref, image_ref, khat_ref, moments_ref, bn_sums_ref, vec_ref, bn_gain_ref,
     forward_ref, to_taps_ref,
-    product_ref, taps_ref,
-    dconv_ref, dhat_ref, all_taps_ref,
+    product_hbm, taps_ref,
+    product_ref, dconv_ref, dhat_ref, all_taps_ref, sems,
 ):
     step = pl.program_id(0)
+
+    def writes(at, images):
+        return [pltpu.make_async_copy(product_ref.at[m], product_hbm.at[4 * at + m], sems.at[m]) for m in images]
+
+    @pl.when(step > 0)
+    def _():
+        wait_all(writes(step - 1, range(4)))
+
     mean, bn_inv = batch_norm_terms(moments_ref, total)
     bn_sums = arrived(bn_sums_ref) * np.float32(1.0 / total)
     gain = as_row(bn_gain_ref) * bn_inv
@@ -561,6 +569,7 @@
                     tap_im.append(xr * gi - xi * gr)
             dhat_ref[re, :] += tree_sum(tap_re)
             dhat_ref[im, :] += tree_sum(tap_im)
+        start_all(writes(step, images))
 
     @pl.when(step == pl.num_programs(0) - 1)
     def _():
@@ -576,6 +585,7 @@
                 taps_ref[i] = all_taps_ref[i * size : (i + 1) * size, :].astype(jnp.bfloat16)
             else:
                 taps_ref[i] = jnp.zeros((size, D), jnp.bfloat16)
+        wait_all(writes(step, range(4)))
 
 
 def gradient_spectra(total, dbn, conv, image_rows, khat, moments, bn_sums, vec, bn_gain, tables):
@@ -585,19 +595,20 @@
     devices = lax.axis_size("dp") * lax.axis_size("mp")
     f32, bf16 = jnp.float32, jnp.bfloat16
     block = pl.BlockSpec((STEP, D), lambda i: (i, 0))
-    spectra = pl.BlockSpec((4, FROWS, 2 * D), lambda i: (i, 0, 0))
     taps = jax.ShapeDtypeStruct((devices, max(8, NTAPS // devices), D), bf16)
     return pl.pallas_call(
         lambda *refs: spectra_kernel(total, *refs),
         grid=(steps,),
         in_specs=[block] * 3
         + [whole(a) for a in (khat, moments, bn_sums, vec, bn_gain, forward, to_taps)],
-        out_specs=[spectra, whole(taps)],
+        out_specs=[pl.BlockSpec(memory_space=pl.ANY), whole(taps)],
         out_shape=[jax.ShapeDtypeStruct((4 * steps, FROWS, 2 * D), bf16), taps],
         scratch_shapes=[
+            pltpu.VMEM((4, FROWS, 2 * D), bf16),
             pltpu.VMEM((STEP, D), bf16),
             pltpu.VMEM((FROWS, D), f32),
             pltpu.VMEM((NTAPS, D), f32),
+            pltpu.SemaphoreType.DMA((4,)),
         ],
         compiler_params=pltpu.CompilerParams(vmem_limit_bytes=VMEM_LIMIT),
         cost_estimate=pl.CostEstimate(

time: 154 us -> 153 us (level)
  no operation moved by 1% of the time
where the time goes in v4:
time: 153 us
  Pallas kernels  78.6 us (51%)
  blocking collectives  23.3 us (15%)
  starting transfers between devices  18.4 us (12%)
  waiting for transfers between devices  14.7 us (10%)
  between operations  14.2 us (9%)
  local copies, waits for them, and re-layouts  2.54 us (2%)
    pallas_call x1, Pallas kernels, mlp(): pl.pallas_call(lambda *refs: mlp_kernel(total, *refs), in_specs=[hbm] * 3...  42.4 us
    all_to_all x2, blocking collectives, exchange(): return lax.all_to_all(x, ('dp', 'mp'), split_axis=0, concat_axis=0)  23.3 us
    pallas_call x1, Pallas kernels, gradient_spectra(): pl.pallas_call(lambda *refs: spectra_kernel(total, *refs), grid=(steps,),...  16.2 us
    ppermute x16, starting transfers between devices, swap(): return lax.ppermute(x, axis, [(i, i ^ bit) for i in range(size)])  15.8 us
    ppermute x16, waiting for transfers between devices, swap(): return lax.ppermute(x, axis, [(i, i ^ bit) for i in range(size)])  12.1 us
    pallas_call x1, Pallas kernels, conv_forward(): pl.pallas_call(conv_kernel, grid=(steps,), in_specs=[pl.BlockSpec((STEP,...  11.5 us
    pallas_call x1, Pallas kernels, image_gradient(): pl.pallas_call(inverse_kernel, grid=(rows // STEP,), in_specs=[pl.BlockSp...  6.68 us
  transfers between devices with their start and end apart: 18, of which 11 were waited for; matrix products, arithmetic and copies ran while one was open for 0% of the time, Pallas kernels for 23%

profile of v4, /device:TPU:0, one launch (start us, length us, event | category | flops | bytes accessed | tf_op | source)
XLA Modules:
  0.0 152.8 jit_solution(2519810334708180632)
XLA Ops:
  7.2 0.0 reduce-scatter.2.cloned.1.call-start
  7.2 1.0 broadcast_select_fusion
  8.2 4.1 %collective-permute-start.1 = (bf16[384,384]{1,0:T(8,128)(2,1)S(1)}, bf16[384,384]{1,0:T(8,128)(2,1)S(1)}, u32[]{:S(2)}, u32[]{:S(2)}) collective-permute-start(bf16[384,384]{1,0:T(8,128)(2,1)S(1)} %broadcast_select_fusion), channel_id=1, source_target_pairs={{0,2},{1,3},{2,0},{3,1},{4,6},{5,7},{6,4},{7,5},{8,10},{9,11},{10,... | collective-permute-start | bytes 884744 | tf_op jit(solution)/shard_map/ppermute | solution.py:712
  12.3 1.6 %collective-permute-start = (bf16[384,384]{1,0:T(8,128)(2,1)S(1)}, bf16[384,384]{1,0:T(8,128)(2,1)S(1)}, u32[]{:S(2)}, u32[]{:S(2)}) collective-permute-start(bf16[384,384]{1,0:T(8,128)(2,1)S(1)} %broadcast_select_fusion), channel_id=1, source_target_pairs={{0,1},{1,0},{2,3},{3,2},{4,5},{5,4},{6,7},{7,6},{8,9},{9,8},{10,11... | collective-permute-start | bytes 884744 | tf_op jit(solution)/shard_map/ppermute | solution.py:712
  13.9 11.5 %conv_forward.1 = (f32[3136,384]{1,0:T(8,128)}, f32[736,384]{1,0:T(8,128)}, f32[32,2,384]{2,1,0:T(2,128)}) custom-call(bf16[3136,384]{1,0:T(8,128)(2,1)} %refs_2_.3, f32[5,51,384]{2,1,0:T(8,128)} %bitcast.7, f32[5,51,384]{2,1,0:T(8,128)} %wide_ref.1, f32[5,5,384]{2,1,0:T(8,128)} %small_ref.1, s32[5,51,384]{2,1,0:T(8,128)} %bitcast.4, s32[5,51,384]{2,1,0:T(8,128)} %refs_9_.4, ...), custom_call_target="tpu_custom_call" | custom-call | flops 3545235456 | bytes 12042240 | tf_op jit(solution)/shard_map/conv_forward/pallas_call | solution.py:194
  25.5 0.3 collective-permute-done.1.refs_14_
  25.8 0.2 collective-permute-done.refs_13_
  26.0 0.0 collective-permute-start.3
  26.0 0.5 collective-permute-start.4
  26.5 1.5 collective-permute-start.2
  28.0 12.7 %all_to_all.15.refs_3_.refs_4_ = f32[32,2,384]{2,1,0:T(2,128)} all-to-all(f32[32,2,384]{2,1,0:T(2,128)} %get-tuple-element.52), channel_id=1, replica_groups=mesh['dp'=8,'mp'=4] {'dp','mp'}, dimensions={0} | all-to-all | bytes 196608 | tf_op jit(solution)/shard_map/all_to_all | solution.py:231
  40.7 0.0 collective-permute-done.4.refs_17_
  40.7 0.0 copy-start.10
  40.7 0.1 collective-permute-start.5
  40.8 1.6 %collective-permute-done.5.refs_18_ = bf16[384,384]{1,0:T(8,128)(2,1)S(1)} collective-permute-done((bf16[384,384]{1,0:T(8,128)(2,1)S(1)}, bf16[384,384]{1,0:T(8,128)(2,1)S(1)}, u32[]{:S(2)}, u32[]{:S(2)}) %collective-permute-start.5) | collective-permute-done | bytes 294944 | tf_op jit(solution)/shard_map/ppermute | solution.py:712
  42.4 0.7 copy-done.11
  43.1 42.4 %mlp.1 = (bf16[3136,384]{1,0:T(8,128)(2,1)}, f32[3136,384]{1,0:T(8,128)}, bf16[8,4,96,384]{3,2,1,0:T(8,128)(2,1)}, f32[32,2,384]{2,1,0:T(2,128)}, f32[8,384]{1,0:T(8,128)}) custom-call(f32[3136,384]{1,0:T(8,128)} %get-tuple-element.51.refs_0_.refs_1_, bf16[3136,384]{1,0:T(8,128)(2,1)} %refs_2_.3, bf16[3136,384]{1,0:T(8,128)(2,1)} %grad_ref.1, ...), custom_call_target="tpu_custom_call" | custom-call | flops 22196256768 | bytes 24084480 | tf_op jit(solution)/shard_map/mlp/pallas_call | solution.py:473
  85.5 0.0 reduce-scatter.2.cloned.1.call-update
  85.5 0.9 copy-done.5
  86.4 10.6 %all_to_all.16.refs_5_.refs_11_ = f32[32,2,384]{2,1,0:T(2,128)} all-to-all(f32[32,2,384]{2,1,0:T(2,128)S(1)} %copy-done.5), channel_id=1, replica_groups=mesh['dp'=8,'mp'=4] {'dp','mp'}, dimensions={0} | all-to-all | bytes 196608 | tf_op jit(solution)/shard_map/all_to_all | solution.py:231
  97.0 16.2 %gradient_spectra.1 = (bf16[8,736,768]{2,1,0:T(8,128)(2,1)}, bf16[32,8,384]{2,1,0:T(8,128)(2,1)}) custom-call(f32[3136,384]{1,0:T(8,128)} %get-tuple-element.63.refs_0_, f32[3136,384]{1,0:T(8,128)} %get-tuple-element.51.refs_0_.refs_1_, bf16[3136,384]{1,0:T(8,128)(2,1)} %refs_2_.3, f32[736,384]{1,0:T(8,128)} %get-tuple-element.64.refs_3_, ...), custom_call_target="tpu_custom_call" | custom-call | flops 1772617728 | bytes 31309824 | tf_op jit(solution)/shard_map/gradient_spectra/pallas_call | solution.py:599
  113.2 2.6 %all-to-all-start.2 = ((bf16[32,8,384]{2,1,0:T(8,128)(2,1)}), bf16[32,8,384]{2,1,0:T(8,128)(2,1)S(1)}, u32[]{:S(2)}, u32[]{:S(2)}) async-start(bf16[32,8,384]{2,1,0:T(8,128)(2,1)} %get-tuple-element.67), calls=%async_computation.2 | async-start | bytes 393216 | tf_op jit(solution)/shard_map/all_to_all | solution.py:231
  115.9 0.0 copy-start.1
  115.9 0.0 copy-start.2
  115.9 0.0 copy-start.4
  115.9 6.7 %image_gradient.1 = bf16[3136,384]{1,0:T(8,128)(2,1)} custom-call(bf16[8,736,768]{2,1,0:T(8,128)(2,1)} %get-tuple-element.68.product_ref, bf16[3136,384]{1,0:T(8,128)(2,1)} %grad_ref.1, bf16[196,736]{1,0:T(8,128)(2,1)} %constant.29.clone.inverse_ref), custom_call_target="tpu_custom_call" | custom-call | flops 1772617728 | bytes 12042240 | tf_op jit(solution)/shard_map/image_gradient/pallas_call | solution.py:631
  122.6 2.6 %all-to-all-done.2.taps_ref = bf16[32,8,384]{2,1,0:T(8,128)(2,1)S(1)} async-done(((bf16[32,8,384]{2,1,0:T(8,128)(2,1)}), bf16[32,8,384]{2,1,0:T(8,128)(2,1)S(1)}, u32[]{:S(2)}, u32[]{:S(2)}) %all-to-all-start.2) | async-done | bytes 196640 | tf_op jit(solution)/shard_map/all_to_all | solution.py:231
  125.2 1.0 copy-done.3
  126.1 0.1 messages.1
  126.2 0.1 collective-permute-start.6
  126.3 2.0 %collective-permute-start.7 = (bf16[104,384]{1,0:T(8,128)(2,1)S(1)}, bf16[104,384]{1,0:T(8,128)(2,1)S(1)}, u32[]{:S(2)}, u32[]{:S(2)}) collective-permute-start(bf16[104,384]{1,0:T(8,128)(2,1)S(1)} %get-tuple-element.74), channel_id=1, source_target_pairs={{0,2},{1,3},{2,0},{3,1},{4,6},{5,7},{6,4},{7,5},{8,10},{9,11},{10,... | collective-permute-start | bytes 239624 | tf_op jit(solution)/shard_map/ppermute | solution.py:712
  128.2 2.4 %collective-permute-start.8 = (bf16[104,384]{1,0:T(8,128)(2,1)S(1)}, bf16[104,384]{1,0:T(8,128)(2,1)S(1)}, u32[]{:S(2)}, u32[]{:S(2)}) collective-permute-start(bf16[104,384]{1,0:T(8,128)(2,1)S(1)} %get-tuple-element.75), channel_id=1, source_target_pairs={{0,3},{1,2},{2,1},{3,0},{4,7},{5,6},{6,5},{7,4},{8,11},{9,10},{10,... | collective-permute-start | bytes 239624 | tf_op jit(solution)/shard_map/ppermute | solution.py:712
  130.7 0.9 collective-permute-done.6.refs_0_
  131.6 4.2 %collective-permute-done.7.refs_1_ = bf16[104,384]{1,0:T(8,128)(2,1)S(1)} collective-permute-done((bf16[104,384]{1,0:T(8,128)(2,1)S(1)}, bf16[104,384]{1,0:T(8,128)(2,1)S(1)}, u32[]{:S(2)}, u32[]{:S(2)}) %collective-permute-start.7) | collective-permute-done | bytes 79904 | tf_op jit(solution)/shard_map/ppermute | solution.py:712
  135.8 0.0 collective-permute-done.8.refs_2_
  135.8 1.4 collective-permute-start.11
  137.2 1.2 collective-permute-start.10
  138.4 1.0 collective-permute-start.9
  139.4 0.0 collective-permute-start.12
  139.4 2.1 %collective-permute-done.11.refs_3_ = bf16[128,384]{1,0:T(8,128)(2,1)S(1)} collective-permute-done((bf16[128,384]{1,0:T(8,128)(2,1)S(1)}, bf16[128,384]{1,0:T(8,128)(2,1)S(1)}, u32[]{:S(2)}, u32[]{:S(2)}) %collective-permute-start.11) | collective-permute-done | bytes 98336 | tf_op jit(solution)/shard_map/ppermute | solution.py:712
  141.5 0.0 collective-permute-start.15
  141.5 1.0 collective-permute-done.10.refs_2_
  142.5 0.0 collective-permute-start.14
  142.5 0.6 collective-permute-done.9.refs_1_
  143.0 0.0 collective-permute-done.12.refs_4_
  143.0 0.7 collective-permute-done.14.refs_6_
  143.8 0.6 collective-permute-done.13.refs_5_
  144.3 1.6 %finish.1 = (f32[5,51,384]{2,1,0:T(8,128)}, f32[5,51,384]{2,1,0:T(8,128)}, f32[5,5,384]{2,1,0:T(8,128)}, f32[384,384]{1,0:T(8,128)}, f32[384,384]{1,0:T(8,128)},...) custom-call(bf16[128,384]{1,0:T(8,128)(2,1)S(1)} %totals.1.refs_0_, ...), custom_call_target="tpu_custom_call" | custom-call | tf_op jit(solution)/shard_map/finish/pallas_call | solution.py:698
  (23 shorter events, 0.1 us)
Async XLA Ops:
  7.2 118.0 %reduce-scatter.2.cloned.1.call-start = ((), (), s32[]{:S(2)}) async-start(), calls=%async_computation.4 | async-start | bytes 2654208 | tf_op jit(solution)/shard_map/reduce_scatter | solution.py:750
  8.2 17.5 %collective-permute-start.1 = (bf16[384,384]{1,0:T(8,128)(2,1)S(1)}, bf16[384,384]{1,0:T(8,128)(2,1)S(1)}, u32[]{:S(2)}, u32[]{:S(2)}) collective-permute-start(bf16[384,384]{1,0:T(8,128)(2,1)S(1)} %broadcast_select_fusion), channel_id=1, source_target_pairs={{0,2},{1,3},{2,0},{3,1},{4,6},{5,7},{6,4},{7,5},{8,10},{9,11},{10,... | collective-permute-start | bytes 884744 | tf_op jit(solution)/shard_map/ppermute | solution.py:712
  12.3 13.6 %collective-permute-start = (bf16[384,384]{1,0:T(8,128)(2,1)S(1)}, bf16[384,384]{1,0:T(8,128)(2,1)S(1)}, u32[]{:S(2)}, u32[]{:S(2)}) collective-permute-start(bf16[384,384]{1,0:T(8,128)(2,1)S(1)} %broadcast_select_fusion), channel_id=1, source_target_pairs={{0,1},{1,0},{2,3},{3,2},{4,5},{5,4},{6,7},{7,6},{8,9},{9,8},{10,11... | collective-permute-start | bytes 884744 | tf_op jit(solution)/shard_map/ppermute | solution.py:712
  25.8 16.6 %copy-start.6 = (bf16[384,384]{1,0:T(8,128)(2,1)}, bf16[384,384]{1,0:T(8,128)(2,1)S(1)}, u32[]{:S(2)}) copy-start(bf16[384,384]{1,0:T(8,128)(2,1)S(1)} %collective-permute-done.1.refs_14_) | copy-start | bytes 884740
  26.0 16.4 %copy-start.7 = (bf16[384,384]{1,0:T(8,128)(2,1)}, bf16[384,384]{1,0:T(8,128)(2,1)S(1)}, u32[]{:S(2)}) copy-start(bf16[384,384]{1,0:T(8,128)(2,1)S(1)} %collective-permute-done.refs_13_) | copy-start | bytes 884740
  26.0 14.7 %collective-permute-start.3 = (bf16[384,384]{1,0:T(8,128)(2,1)S(1)}, bf16[384,384]{1,0:T(8,128)(2,1)S(1)}, u32[]{:S(2)}, u32[]{:S(2)}) collective-permute-start(bf16[384,384]{1,0:T(8,128)(2,1)S(1)} %collective-permute-done.refs_13_), channel_id=1, source_target_pairs={{0,4},{4,0},{8,12},{12,8},{16,20},{20,16},{24,28},{28,24},{1,5},{5... | collective-permute-start | bytes 884744 | tf_op jit(solution)/shard_map/ppermute | solution.py:712
  26.0 14.7 %collective-permute-start.4 = (bf16[384,384]{1,0:T(8,128)(2,1)S(1)}, bf16[384,384]{1,0:T(8,128)(2,1)S(1)}, u32[]{:S(2)}, u32[]{:S(2)}) collective-permute-start(bf16[384,384]{1,0:T(8,128)(2,1)S(1)} %collective-permute-done.1.refs_14_), channel_id=1, source_target_pairs={{0,4},{4,0},{8,12},{12,8},{16,20},{20,16},{24,28},{28,24},{1,5},{5... | collective-permute-start | bytes 884744 | tf_op jit(solution)/shard_map/ppermute | solution.py:712
  26.5 14.2 %collective-permute-start.2 = (bf16[384,384]{1,0:T(8,128)(2,1)S(1)}, bf16[384,384]{1,0:T(8,128)(2,1)S(1)}, u32[]{:S(2)}, u32[]{:S(2)}) collective-permute-start(bf16[384,384]{1,0:T(8,128)(2,1)S(1)} %collective-permute-done.1.refs_14_), channel_id=1, source_target_pairs={{0,1},{1,0},{2,3},{3,2},{4,5},{5,4},{6,7},{7,6},{8,9},{9,8},{10,11... | collective-permute-start | bytes 884744 | tf_op jit(solution)/shard_map/ppermute | solution.py:712
  40.7 1.7 %copy-start.8 = (bf16[384,384]{1,0:T(8,128)(2,1)}, bf16[384,384]{1,0:T(8,128)(2,1)S(1)}, u32[]{:S(2)}) copy-start(bf16[384,384]{1,0:T(8,128)(2,1)S(1)} %collective-permute-done.3.refs_16_) | copy-start | bytes 884740
  40.7 1.7 %copy-start.9 = (bf16[384,384]{1,0:T(8,128)(2,1)}, bf16[384,384]{1,0:T(8,128)(2,1)S(1)}, u32[]{:S(2)}) copy-start(bf16[384,384]{1,0:T(8,128)(2,1)S(1)} %collective-permute-done.4.refs_17_) | copy-start | bytes 884740
  40.7 1.7 %copy-start.10 = (bf16[384,384]{1,0:T(8,128)(2,1)}, bf16[384,384]{1,0:T(8,128)(2,1)S(1)}, u32[]{:S(2)}) copy-start(bf16[384,384]{1,0:T(8,128)(2,1)S(1)} %collective-permute-done.2.refs_15_) | copy-start | bytes 884740
  40.7 1.6 %collective-permute-start.5 = (bf16[384,384]{1,0:T(8,128)(2,1)S(1)}, bf16[384,384]{1,0:T(8,128)(2,1)S(1)}, u32[]{:S(2)}, u32[]{:S(2)}) collective-permute-start(bf16[384,384]{1,0:T(8,128)(2,1)S(1)} %collective-permute-done.2.refs_15_), channel_id=1, source_target_pairs={{0,4},{4,0},{8,12},{12,8},{16,20},{20,16},{24,28},{28,24},{1,5},{5... | collective-permute-start | bytes 884744 | tf_op jit(solution)/shard_map/ppermute | solution.py:712
  42.4 0.7 copy-start.11
  85.5 0.9 copy-start.5
  113.2 11.9 %all-to-all-start.2 = ((bf16[32,8,384]{2,1,0:T(8,128)(2,1)}), bf16[32,8,384]{2,1,0:T(8,128)(2,1)S(1)}, u32[]{:S(2)}, u32[]{:S(2)}) async-start(bf16[32,8,384]{2,1,0:T(8,128)(2,1)} %get-tuple-element.67), calls=%async_computation.2 | async-start | bytes 393216 | tf_op jit(solution)/shard_map/all_to_all | solution.py:231
  115.9 28.5 %copy-start = (f32[32,2,384]{2,1,0:T(2,128)S(1)}, f32[32,2,384]{2,1,0:T(2,128)}, u32[]{:S(2)}) copy-start(f32[32,2,384]{2,1,0:T(2,128)} %all_to_all.16.refs_5_.refs_11_) | copy-start | bytes 294916
  115.9 28.5 %copy-start.1 = (s32[51,5,384]{2,0,1:T(8,128)S(1)}, s32[51,5,384]{2,0,1:T(8,128)}, u32[]{:S(2)}) copy-start(s32[51,5,384]{2,0,1:T(8,128)} %param.25) | copy-start | bytes 1175044
  115.9 28.5 %copy-start.2 = (s32[5,51,384]{2,1,0:T(8,128)S(1)}, s32[5,51,384]{2,1,0:T(8,128)}, u32[]{:S(2)}) copy-start(s32[5,51,384]{2,1,0:T(8,128)} %refs_9_.4) | copy-start | bytes 1175044
  115.9 28.4 %copy-start.4 = (s32[5,5,384]{2,1,0:T(8,128)S(1)}, s32[5,5,384]{2,1,0:T(8,128)}, u32[]{:S(2)}) copy-start(s32[5,5,384]{2,1,0:T(8,128)} %refs_10_.3) | copy-start | bytes 115204
  125.2 1.0 copy-start.3
  126.2 5.4 %collective-permute-start.6 = (bf16[104,384]{1,0:T(8,128)(2,1)S(1)}, bf16[104,384]{1,0:T(8,128)(2,1)S(1)}, u32[]{:S(2)}, u32[]{:S(2)}) collective-permute-start(bf16[104,384]{1,0:T(8,128)(2,1)S(1)} %get-tuple-element.73), channel_id=1, source_target_pairs={{0,1},{1,0},{2,3},{3,2},{4,5},{5,4},{6,7},{7,6},{8,9},{9,8},{10,11... | collective-permute-start | bytes 239624 | tf_op jit(solution)/shard_map/ppermute | solution.py:712
  126.3 9.5 %collective-permute-start.7 = (bf16[104,384]{1,0:T(8,128)(2,1)S(1)}, bf16[104,384]{1,0:T(8,128)(2,1)S(1)}, u32[]{:S(2)}, u32[]{:S(2)}) collective-permute-start(bf16[104,384]{1,0:T(8,128)(2,1)S(1)} %get-tuple-element.74), channel_id=1, source_target_pairs={{0,2},{1,3},{2,0},{3,1},{4,6},{5,7},{6,4},{7,5},{8,10},{9,11},{10,... | collective-permute-start | bytes 239624 | tf_op jit(solution)/shard_map/ppermute | solution.py:712
  128.2 7.5 %collective-permute-start.8 = (bf16[104,384]{1,0:T(8,128)(2,1)S(1)}, bf16[104,384]{1,0:T(8,128)(2,1)S(1)}, u32[]{:S(2)}, u32[]{:S(2)}) collective-permute-start(bf16[104,384]{1,0:T(8,128)(2,1)S(1)} %get-tuple-element.75), channel_id=1, source_target_pairs={{0,3},{1,2},{2,1},{3,0},{4,7},{5,6},{6,5},{7,4},{8,11},{9,10},{10,... | collective-permute-start | bytes 239624 | tf_op jit(solution)/shard_map/ppermute | solution.py:712
  135.8 5.6 %collective-permute-start.11 = (bf16[128,384]{1,0:T(8,128)(2,1)S(1)}, bf16[128,384]{1,0:T(8,128)(2,1)S(1)}, u32[]{:S(2)}, u32[]{:S(2)}) collective-permute-start(bf16[128,384]{1,0:T(8,128)(2,1)S(1)} %totals.1.refs_0_), channel_id=1, source_target_pairs={{0,24},{4,28},{8,16},{12,20},{16,8},{20,12},{24,0},{28,4},{1,25},{... | collective-permute-start | bytes 294920 | tf_op jit(solution)/shard_map/ppermute | solution.py:712
  137.2 5.2 %collective-permute-start.10 = (bf16[128,384]{1,0:T(8,128)(2,1)S(1)}, bf16[128,384]{1,0:T(8,128)(2,1)S(1)}, u32[]{:S(2)}, u32[]{:S(2)}) collective-permute-start(bf16[128,384]{1,0:T(8,128)(2,1)S(1)} %totals.1.refs_0_), channel_id=1, source_target_pairs={{0,16},{4,20},{8,24},{12,28},{16,0},{20,4},{24,8},{28,12},{1,17},{... | collective-permute-start | bytes 294920 | tf_op jit(solution)/shard_map/ppermute | solution.py:712
  138.4 4.6 %collective-permute-start.9 = (bf16[128,384]{1,0:T(8,128)(2,1)S(1)}, bf16[128,384]{1,0:T(8,128)(2,1)S(1)}, u32[]{:S(2)}, u32[]{:S(2)}) collective-permute-start(bf16[128,384]{1,0:T(8,128)(2,1)S(1)} %totals.1.refs_0_), channel_id=1, source_target_pairs={{0,8},{4,12},{8,0},{12,4},{16,24},{20,28},{24,16},{28,20},{1,9},{5... | collective-permute-start | bytes 294920 | tf_op jit(solution)/shard_map/ppermute | solution.py:712
  139.4 3.6 %collective-permute-start.12 = (bf16[128,384]{1,0:T(8,128)(2,1)S(1)}, bf16[128,384]{1,0:T(8,128)(2,1)S(1)}, u32[]{:S(2)}, u32[]{:S(2)}) collective-permute-start(bf16[128,384]{1,0:T(8,128)(2,1)S(1)} %totals.1.refs_0_), channel_id=1, source_target_pairs={{0,4},{4,0},{8,12},{12,8},{16,20},{20,16},{24,28},{28,24},{1,5},{5... | collective-permute-start | bytes 294920 | tf_op jit(solution)/shard_map/ppermute | solution.py:712
  141.5 1.6 %collective-permute-start.15 = (bf16[128,384]{1,0:T(8,128)(2,1)S(1)}, bf16[128,384]{1,0:T(8,128)(2,1)S(1)}, u32[]{:S(2)}, u32[]{:S(2)}) collective-permute-start(bf16[128,384]{1,0:T(8,128)(2,1)S(1)} %collective-permute-done.11.refs_3_), channel_id=1, source_target_pairs={{0,4},{4,0},{8,12},{12,8},{16,20},{20,16},{24,28},{28,24},{1,5},{5... | collective-permute-start | bytes 294920 | tf_op jit(solution)/shard_map/ppermute | solution.py:712
  142.5 1.3 collective-permute-start.14
  143.0 1.3 collective-permute-start.13
Sparse Core Ops, SparseCore 0:
  85.7 28.5 reduce-scatter.1
